TPU v7x, 128 devices: a whole 4x4x4 slice. The times are simulated.
128 devices in a mesh: node: 16 (over z, y), local: 8 (over x, core).
Axes of the slice: x: 4, y: 4, z: 4, core: 2. Of those that a mesh axis runs over, the one named last changes fastest.
Arguments:
- tokens: bfloat16 [16384, 3584], P(('node', 'local')), may hold values from -6 to 6
- grad_out: bfloat16 [16384, 3584], P(('node', 'local')), may hold values from -6 to 6
- expert_ids: int32 [16384, 8], P(('node', 'local')), may hold values from 0 to 127, as said below
- gate_weights: float32 [16384, 8], P(('node', 'local')), may hold values from 0.08 to 0.8
- w_gate: bfloat16 [128, 3584, 1024], P(('node', 'local')), may hold values from -0.09375 to 0.09375
- w_up: bfloat16 [128, 3584, 1024], P(('node', 'local')), may hold values from -0.09375 to 0.09375
- w_down: bfloat16 [128, 1024, 3584], P(('node', 'local')), may hold values from -0.09375 to 0.09375
Outputs:
- token_grads: bfloat16 [16384, 3584], P(('node', 'local'))
Inputs may be any that keep to these rules, and one draw needn't show every extreme that they name: `expert_ids`: each row names 8 different experts; expert e belongs to node group e // 8, and the experts of one row lie in at most 4 node groups.
All inputs are finite; a program needn't handle non-finite values.
Results may differ from a plain program's by a relative error of at most 0.0057.
Values may be sent and summed in bfloat16 or wider, within the bound.
No kernel may reach another device: no remote copies, remote signals or barrier semaphores. Data moves between devices by JAX's collectives and lax.ppermute only.
A program may use at most 128 MiB of HBM per device.

v0:
```python
import jax
import jax.numpy as jnp
from jax import lax
from jax.sharding import PartitionSpec as P


def slot_layout(expert_ids, expert_total, capacity):
    routes = expert_ids.reshape(-1)
    onehot = (routes[:, None] == jnp.arange(expert_total, dtype=jnp.int32)[None, :]).astype(
        jnp.int32
    )
    route_rank = jnp.sum((jnp.cumsum(onehot, axis=0) - onehot) * onehot, axis=1)
    kept_route = route_rank < capacity
    slot_index = jnp.where(kept_route, routes * capacity + route_rank, -1)
    return (slot_index.reshape(expert_ids.shape), kept_route.reshape(expert_ids.shape))


def expert_rows(packed, w_gate, w_up, w_down):
    model_width = w_gate.shape[1]
    sources, experts, slot_rows, _ = packed.shape
    flattened = jnp.moveaxis(packed, 1, 0).reshape(experts, sources * slot_rows, 2 * model_width)
    inputs = flattened[:, :, :model_width]
    upstream = flattened[:, :, model_width:]
    gate_pre = jnp.einsum("erd,edf->erf", inputs, w_gate, preferred_element_type=jnp.float32)
    up_pre = jnp.einsum("erd,edf->erf", inputs, w_up, preferred_element_type=jnp.float32)
    hidden_grad = jnp.einsum("erd,efd->erf", upstream, w_down, preferred_element_type=jnp.float32)
    sigmoid_gate = jax.nn.sigmoid(gate_pre)
    up_grad = (hidden_grad * gate_pre * sigmoid_gate).astype(jnp.bfloat16)
    gate_grad = (
        hidden_grad * up_pre * sigmoid_gate * (1.0 + gate_pre * (1.0 - sigmoid_gate))
    ).astype(jnp.bfloat16)
    summed = jnp.einsum("erf,edf->erd", gate_grad, w_gate, preferred_element_type=jnp.float32)
    summed = summed + jnp.einsum("erf,edf->erd", up_grad, w_up, preferred_element_type=jnp.float32)
    result = summed.astype(jnp.bfloat16).reshape(experts, sources, slot_rows, model_width)
    return jnp.moveaxis(result, 0, 1)


def shards(tokens, grad_out, expert_ids, gate_weights, w_gate, w_up, w_down):
    tok_rows, model_width = tokens.shape
    chosen = expert_ids.shape[1]
    devices_all = lax.axis_size(("node", "local"))
    local_experts = w_gate.shape[0]
    expert_total = local_experts * devices_all
    capacity = max(2, 3 * tok_rows * chosen // (4 * expert_total))
    slot_index, kept_route = slot_layout(expert_ids, expert_total, capacity)
    slot_iota = jnp.arange(expert_total * capacity, dtype=jnp.int32)
    joined = jnp.concatenate([tokens, grad_out], axis=1)
    dispatch_matrix = jnp.sum(
        (slot_index[:, :, None] == slot_iota[None, None, :]).astype(jnp.bfloat16), axis=1
    )
    packed = lax.dot_general(
        dispatch_matrix, joined, (((0,), (0,)), ((), ())), preferred_element_type=jnp.float32
    ).astype(jnp.bfloat16)
    packed = packed.reshape(devices_all, local_experts, capacity, 2 * model_width)
    arrived = lax.all_to_all(packed, ("node", "local"), split_axis=0, concat_axis=0, tiled=True)
    result = expert_rows(arrived, w_gate, w_up, w_down)
    returned = lax.all_to_all(result, ("node", "local"), split_axis=0, concat_axis=0, tiled=True)
    returned = returned.reshape(expert_total * capacity, model_width)
    safe_slot = jnp.where(kept_route, slot_index, 0)
    route_grads = returned[safe_slot]
    weight = jnp.where(kept_route, gate_weights, 0.0)
    combined = jnp.sum(route_grads.astype(jnp.float32) * weight[:, :, None], axis=1)
    return combined.astype(jnp.bfloat16)


def solution(mesh):
    placed = (
        P(("node", "local"), None),
        P(("node", "local"), None),
        P(("node", "local"), None),
        P(("node", "local"), None),
        P(("node", "local"), None, None),
        P(("node", "local"), None, None),
        P(("node", "local"), None, None),
    )
    return jax.shard_map(
        shards, mesh=mesh, in_specs=placed, out_specs=P(("node", "local"), None), check_vma=False
    )
```

profile of v0, /device:TPU:1, one launch (start us, length us, event | category | flops | bytes accessed | tf_op | source)
XLA Modules:
  0.0 407.9 jit_solution(8638217609773334749)
XLA Ops:
  0.0 0.7 broadcast_multiply_fusion
  0.7 0.8 copy.26
  1.5 0.1 eq.42
  1.6 0.1 eq.38
  1.7 0.1 copy.31
  1.8 0.1 copy.28
  1.9 0.2 fusion.23
  2.2 0.1 copy.29
  2.3 0.4 fusion.22
  2.6 0.1 reduce_sum.33
  2.8 1.0 fusion.19
  3.8 7.2 %convolution_convert_fusion = bf16[768,7168]{1,0:T(8,128)(2,1)} fusion(bf16[128,768]{1,0:T(8,128)(2,1)S(1)} %fusion.19, bf16[128,3584]{1,0:T(8,128)(2,1)} %param.8, bf16[128,3584]{1,0:T(8,128)(2,1)} %param.7), kind=kOutput, calls=%fused_computation.3 | convolution fusion | flops 1418461184 | bytes 13041664 | tf_op jit(solution)/shard_map/dot_general | solution.py:51
  10.9 15.9 %reshape.83 = bf16[128,1,6,7168]{3,2,0,1:T(8,128)(2,1)} reshape(bf16[768,7168]{1,0:T(8,128)(2,1)} %convolution_convert_fusion) | data formatting | bytes 22020096 | tf_op jit(solution)/shard_map/reshape | solution.py:54
  26.8 177.0 %all_to_all.10 = bf16[128,1,6,7168]{3,2,1,0:T(8,128)(2,1)} all-to-all(bf16[128,1,6,7168]{3,2,1,0:T(8,128)(2,1)} %bitcast.43), channel_id=1, replica_groups=mesh['node'=16,'local'=8] {'node','local'}, dimensions={0} | all-to-all | bytes 22020096 | tf_op jit(solution)/shard_map/all_to_all | solution.py:55
  203.8 16.5 %reshape_transpose.3 = bf16[1,768,7168]{2,1,0:T(8,128)(2,1)} reshape(bf16[128,1,6,7168]{3,2,1,0:T(8,128)(2,1)} %all_to_all.10) | data formatting | bytes 22020096 | tf_op jit(solution)/shard_map/reshape;transpose | solution.py:21
  220.3 0.0 copy-start
  220.3 0.0 slice-start
  220.3 9.8 %fusion.3 = f32[768,1024]{1,0:T(8,128)S(1)} fusion(bf16[1,3584,1024]{2,1,0:T(8,128)(2,1)} %param.11, bf16[1,768,7168]{2,1,0:T(8,128)(2,1)} %reshape_transpose.3), kind=kOutput, calls=%fused_computation.7 | convolution fusion | flops 5637144576 | bytes 15990784 | tf_op jit(solution)/shard_map/erd,edf->erf/dot_general | solution.py:24
  230.1 0.0 copy-done
  230.1 0.0 slice-start.1
  230.1 8.3 %fusion.9 = f32[768,1024]{1,0:T(8,128)S(1)} fusion(bf16[1,1024,3584]{2,1,0:T(8,128)(2,1)} %param.13, bf16[1,768,7168]{2,1,0:T(8,128)(2,1)S(1)} %copy-done), kind=kOutput, calls=%fused_computation.13 | convolution fusion | flops 5637144576 | bytes 15990784 | tf_op jit(solution)/shard_map/erd,efd->erf/dot_general | solution.py:26
  238.4 8.8 %multiply_convert_fusion.1 = bf16[768,1024]{1,0:T(8,128)(2,1)S(1)} fusion(f32[768,1024]{1,0:T(8,128)S(1)} %fusion.3, f32[768,1024]{1,0:T(8,128)S(1)} %fusion.9, bf16[1,3584,1024]{2,1,0:T(8,128)(2,1)} %param.12, bf16[1,768,7168]{2,1,0:T(8,128)(2,1)S(1)} %copy-done), kind=kOutput, calls=%fused_computation.18 | convolution fusion | flops 5645008896 | bytes 20709376 | tf_op jit(solution)/shard_map/erd,edf->erf/dot_general | solution.py:25
  247.3 0.0 slice-done
  247.3 0.0 slice-done.1
  247.3 8.6 %fusion.1 = f32[768,3584]{1,0:T(8,128)} fusion(bf16[768,1024]{1,0:T(8,128)(2,1)S(1)} %multiply_convert_fusion.1, bf16[1,3584,1024]{2,1,0:T(8,128)(2,1)S(1)} %bitcast.46), kind=kOutput, calls=%fused_computation.5 | convolution fusion | flops 5637144576 | bytes 19922944 | tf_op jit(solution)/shard_map/erf,edf->erd/dot_general | solution.py:32
  255.9 12.4 %add_convert_fusion = bf16[768,3584]{1,0:T(8,128)(2,1)} fusion(f32[768,3584]{1,0:T(8,128)} %fusion.1, bf16[1,3584,1024]{2,1,0:T(8,128)(2,1)} %param.12, f32[768,1024]{1,0:T(8,128)S(1)} %fusion.9, f32[768,1024]{1,0:T(8,128)S(1)} %fusion.3), kind=kOutput, calls=%fused_computation.4 | convolution fusion | flops 5647368192 | bytes 30146560 | tf_op jit(solution)/shard_map/erf,edf->erd/dot_general | solution.py:33
  268.4 9.6 %transpose_reshape.3 = bf16[128,1,6,3584]{3,2,0,1:T(8,128)(2,1)} reshape(bf16[768,3584]{1,0:T(8,128)(2,1)} %add_convert_fusion) | data formatting | bytes 11010048 | tf_op jit(solution)/shard_map/transpose;reshape | solution.py:35
  278.0 0.0 copy-start.1
  278.0 5.7 %all-to-all-start.1 = ((bf16[128,1,6,3584]{3,2,1,0:T(8,128)(2,1)}), bf16[128,1,6,3584]{3,2,1,0:T(8,128)(2,1)}, u32[]{:S(2)}, u32[]{:S(2)}) async-start(bf16[128,1,6,3584]{3,2,1,0:T(8,128)(2,1)} %bitcast.44), calls=%async_computation.1 | async-start | bytes 14680064 | tf_op jit(solution)/shard_map/all_to_all | solution.py:57
  283.6 0.0 copy-done.1
  283.6 0.1 copy.34
  283.7 0.1 reshape.92
  283.9 86.6 %all-to-all-done.1 = bf16[128,1,6,3584]{3,2,1,0:T(8,128)(2,1)} async-done(((bf16[128,1,6,3584]{3,2,1,0:T(8,128)(2,1)}), bf16[128,1,6,3584]{3,2,1,0:T(8,128)(2,1)}, u32[]{:S(2)}, u32[]{:S(2)}) %all-to-all-start.1) | async-done | bytes 5505056 | tf_op jit(solution)/shard_map/all_to_all | solution.py:57
  370.5 9.7 %reshape.89 = bf16[768,3584]{1,0:T(8,128)(2,1)} reshape(bf16[128,1,6,3584]{3,2,1,0:T(8,128)(2,1)} %all-to-all-done.1) | data formatting | bytes 11010048 | tf_op jit(solution)/shard_map/reshape | solution.py:58
  380.1 17.1 %gather_fusion = bf16[1024,3584]{1,0:T(8,128)(2,1)} fusion(bf16[768,3584]{1,0:T(8,128)(2,1)} %reshape.89, s32[1024]{0:T(1024)S(1)} %broadcast_clamp_fusion), kind=kCustom, calls=%fused_computation | custom fusion | bytes 14684160 | tf_op jit(solution)/shard_map/gather | solution.py:60
  397.2 10.7 %fusion = bf16[128,3584]{1,0:T(8,128)(2,1)} fusion(bf16[1024,3584]{1,0:T(8,128)(2,1)} %gather_fusion, f32[128,8]{1,0:T(8,128)S(1)} %broadcast_select_fusion), kind=kLoop, calls=%fused_computation.2 | loop fusion | flops 10551296 | bytes 8261632 | tf_op jit(solution)/shard_map/reduce_sum | solution.py:62
  (8 shorter events, 0.1 us)
Async XLA Ops:
  220.3 9.9 %copy-start = (bf16[1,768,7168]{2,1,0:T(8,128)(2,1)S(1)}, bf16[1,768,7168]{2,1,0:T(8,128)(2,1)}, u32[]{:S(2)}) copy-start(bf16[1,768,7168]{2,1,0:T(8,128)(2,1)} %reshape_transpose.3) | copy-start | bytes 33030148
  220.3 27.0 %slice-start = ((s8[7340032]{0:T(1024)(128)(4,1)}), s8[4194304]{0:T(1024)(128)(4,1)S(1)}, s32[]{:S(2)}) async-start(s8[7340032]{0:T(1024)(128)(4,1)} %bitcast.45), calls=%async_computation.2 | async-start | bytes 8388608
  230.1 17.2 %slice-start.1 = ((s8[7340032]{0:T(1024)(128)(4,1)}), s8[3145728]{0:T(1024)(128)(4,1)S(1)}, s32[]{:S(2)}) async-start(s8[7340032]{0:T(1024)(128)(4,1)} %bitcast.45), calls=%async_computation.3 | async-start | bytes 6291456
  278.0 5.7 %copy-start.1 = (f32[128,8]{0,1:T(8,128)S(1)}, f32[128,8]{0,1:T(8,128)}, u32[]{:S(2)}) copy-start(f32[128,8]{0,1:T(8,128)} %param.10) | copy-start | bytes 12292
  278.0 92.5 %all-to-all-start.1 = ((bf16[128,1,6,3584]{3,2,1,0:T(8,128)(2,1)}), bf16[128,1,6,3584]{3,2,1,0:T(8,128)(2,1)}, u32[]{:S(2)}, u32[]{:S(2)}) async-start(bf16[128,1,6,3584]{3,2,1,0:T(8,128)(2,1)} %bitcast.44), calls=%async_computation.1 | async-start | bytes 14680064 | tf_op jit(solution)/shard_map/all_to_all | solution.py:57
where the time goes:
time: 410 us; the launch traced here: 408 us
  blocking collectives  177 us (43%)
  waiting for transfers between devices  86.6 us (21%)
  local copies, waits for them, and re-layouts  70.3 us (17%)
  matrix products  55.2 us (13%)
  other arithmetic  13.1 us (3%)
  starting transfers between devices  5.67 us (1%)
    all_to_all x1, blocking collectives, shards(): lax.all_to_all(packed, ('node', 'local'), split_axis=0, concat_axis=0, ti...  177 us
    all_to_all x1, waiting for transfers between devices, shards(): lax.all_to_all(result, ('node', 'local'), split_axis=0, concat_axis=0, ti...  86.6 us
    gather x1, local copies, waits for them, and re-layouts, shards(): route_grads = returned[safe_slot]  17.1 us
    another operation x1, local copies, waits for them, and re-layouts, expert_rows(): jnp.moveaxis(packed, 1, 0)  16.5 us
    reshape x1, local copies, waits for them, and re-layouts, shards(): packed.reshape(devices_all, local_experts, capacity, 2 * model_width)  15.9 us
    dot_general x1, matrix products, expert_rows(): jnp.einsum('erf,edf->erd', up_grad, w_up, preferred_element_type=jnp.floa...  12.4 us
    reduce_sum x1, other arithmetic, shards(): jnp.sum(route_grads.astype(jnp.float32) * weight[:, :, None], axis=1)  10.7 us
    dot_general x1, matrix products, expert_rows(): jnp.einsum('erd,edf->erf', inputs, w_gate, preferred_element_type=jnp.flo...  9.84 us
  transfers between devices with their start and end apart: 1, of which 1 were waited for; matrix products, arithmetic and copies ran while one was open for 0% of the time, Pallas kernels for 0%

commit v1 on v0

v1 whole, which is shorter than its diff:
```python
import functools

import jax
import jax.numpy as jnp
from jax import lax
from jax.experimental import pallas as pl
from jax.experimental.pallas import tpu as pltpu
from jax.sharding import PartitionSpec as P

AXES = ("node", "local")
D = 3584
FF = 1024
TOP = 8
TOK = 128
EXPERTS = 128
UNIT = 896
GROUP = 256
SRC = 32
MIB = 1 << 20

PARTS = ((4, 0), (2, 4))


def iota(shape, dim):
    return lax.broadcasted_iota(jnp.int32, shape, dim)


def one(mask):
    return jnp.where(mask, 1.0, 0.0)


def ranked(ids):
    lanes = iota((TOK, EXPERTS), 1)
    chosen = jnp.zeros((TOK, EXPERTS), jnp.float32)
    for k in range(TOP):
        chosen = chosen + one(ids[:, k : k + 1] == lanes)
    earlier = one(iota((TOK, TOK), 1) < iota((TOK, TOK), 0))
    rank = jnp.dot(
        earlier.astype(jnp.bfloat16), chosen.astype(jnp.bfloat16), preferred_element_type=jnp.float32
    )
    return jnp.where(chosen > 0.5, rank, 64.0)


def pack_kernel(c, first, ids_ref, *refs):
    chunks = 8 // c
    x_refs, out_ref, onehot = refs[:chunks], refs[chunks], refs[chunks + 1]

    @pl.when(pl.program_id(0) == 0)
    def _():
        rank = ranked(ids_ref[...]).T.astype(jnp.bfloat16)
        rows = EXPERTS * 8
        spread = one(iota((rows, EXPERTS), 0) // 8 == iota((rows, EXPERTS), 1)).astype(jnp.bfloat16)
        rank = jnp.dot(spread, rank, preferred_element_type=jnp.float32).astype(jnp.int32)
        r = iota((rows, TOK), 0) % 8
        hit = rank == first + r % c
        for a in range(chunks):
            onehot[:, a * TOK : (a + 1) * TOK] = one(hit & (r // c == a)).astype(jnp.bfloat16)

    x = jnp.concatenate([ref[...] for ref in x_refs], axis=0)
    out_ref[...] = jnp.dot(onehot[...], x, preferred_element_type=jnp.float32).astype(jnp.bfloat16)


def pack(c, first, ids, tokens, grads):
    chunks = 8 // c
    specs, operands = [pl.BlockSpec((TOK, TOP), lambda i: (0, 0))], [ids]
    for a in range(chunks):
        start = a % (chunks // 2) * c
        specs.append(pl.BlockSpec((TOK, UNIT), lambda i, start=start: (0, start + i)))
        operands.append(tokens if a < chunks // 2 else grads)
    rows = EXPERTS * 8
    return pl.pallas_call(
        functools.partial(pack_kernel, c, first),
        grid=(c,),
        in_specs=specs,
        out_specs=pl.BlockSpec((rows, UNIT), lambda i: (0, i)),
        out_shape=jax.ShapeDtypeStruct((rows, c * UNIT), jnp.bfloat16),
        scratch_shapes=[pltpu.VMEM((rows, chunks * TOK), jnp.bfloat16)],
        compiler_params=pltpu.CompilerParams(vmem_limit_bytes=20 * MIB),
        cost_estimate=pl.CostEstimate(
            flops=2 * rows * chunks * TOK * c * UNIT, bytes_accessed=rows * c * UNIT * 2, transcendentals=0
        ),
        name="pack_slots",
    )(*operands)


def sorter(c):
    row, col = iota((GROUP, GROUP), 0), iota((GROUP, GROUP), 1)
    per_chunk = SRC * c
    inner = row % per_chunk
    return one(col == inner // c * 8 + row // per_chunk * c + inner % c).astype(jnp.bfloat16)


def unsorter(c):
    row, col = iota((GROUP, GROUP), 1), iota((GROUP, GROUP), 0)
    per_chunk = SRC * c
    inner = row % per_chunk
    return one(col == inner // c * 8 + row // per_chunk * c + inner % c).astype(jnp.bfloat16)


def ffn_kernel(c, out_at, wire_ref, wg_hbm, wu_hbm, wd_hbm, *refs):
    if out_at:
        refs = refs[1:]
    out_hbm, wg, wu, wd, x, up_g, gate_g, res, out, sems, out_sem = refs
    chunks, per_chunk = 8 // c, SRC * c
    width = c * UNIT
    step = 256
    blocks = FF // step

    def loads(j):
        cols = pl.ds(pl.multiple_of(j * step, step), step)
        return (
            pltpu.make_async_copy(wg_hbm.at[:, cols], wg.at[:, cols], sems.at[0, j]),
            pltpu.make_async_copy(wu_hbm.at[:, cols], wu.at[:, cols], sems.at[1, j]),
            pltpu.make_async_copy(wd_hbm.at[cols, :], wd.at[cols, :], sems.at[2, j]),
        )

    for j in range(blocks):
        for copy in loads(j):
            copy.start()

    sort = sorter(c)

    @pl.loop(0, EXPERTS // SRC)
    def _(g):
        rows_in = pl.ds(pl.multiple_of(g * GROUP, GROUP), GROUP)
        rows_x = pl.ds(pl.multiple_of(g * per_chunk, per_chunk), per_chunk)
        for u in range(c):
            part = jnp.dot(
                sort, wire_ref[rows_in, u * UNIT : (u + 1) * UNIT], preferred_element_type=jnp.float32
            ).astype(jnp.bfloat16)
            for a in range(chunks):
                at = a * width + u * UNIT
                x[rows_x, at : at + UNIT] = part[a * per_chunk : (a + 1) * per_chunk]

    @pl.loop(0, blocks)
    def _(j):
        for copy in loads(j):
            copy.wait()
        cols = pl.ds(pl.multiple_of(j * step, step), step)
        gate_pre = jnp.dot(x[:, :D], wg[:, cols], preferred_element_type=jnp.float32)
        up_pre = jnp.dot(x[:, :D], wu[:, cols], preferred_element_type=jnp.float32)
        hidden = lax.dot_general(
            x[:, D:], wd[cols, :], (((1,), (1,)), ((), ())), preferred_element_type=jnp.float32
        )
        s = jax.nn.sigmoid(gate_pre)
        up_g[:, cols] = (hidden * gate_pre * s).astype(jnp.bfloat16)
        gate_g[:, cols] = (hidden * up_pre * s * (1.0 + gate_pre * (1.0 - s))).astype(jnp.bfloat16)

    @pl.loop(0, D // 512)
    def _(j):
        cols = pl.ds(pl.multiple_of(j * 512, 512), 512)
        nt = (((1,), (1,)), ((), ()))
        total = lax.dot_general(gate_g[...], wg[cols, :], nt, preferred_element_type=jnp.float32)
        total = total + lax.dot_general(up_g[...], wu[cols, :], nt, preferred_element_type=jnp.float32)
        res[:, cols] = total.astype(jnp.bfloat16)

    unsort = unsorter(c)
    back = width // 2

    @pl.loop(0, EXPERTS // SRC)
    def _(g):
        rows_out = pl.ds(pl.multiple_of(g * GROUP, GROUP), GROUP)
        rows_x = pl.ds(pl.multiple_of(g * per_chunk, per_chunk), per_chunk)
        stack = jnp.concatenate([res[rows_x, a * back : (a + 1) * back] for a in range(chunks)], axis=0)
        out[rows_out, :] = jnp.dot(unsort, stack, preferred_element_type=jnp.float32).astype(jnp.bfloat16)

    done = pltpu.make_async_copy(out, out_hbm.at[:, pl.ds(out_at, back)], out_sem)
    done.start()
    done.wait()


def ffn(c, out_at, wire, w_gate, w_up, w_down, result=None):
    rows, back = EXPERTS * c, c * UNIT // 2
    wire_rows = EXPERTS * 8
    any_spec = pl.BlockSpec(memory_space=pl.ANY)
    operands = [wire, w_gate, w_up, w_down] + ([] if result is None else [result])
    return pl.pallas_call(
        functools.partial(ffn_kernel, c, out_at),
        in_specs=[pl.BlockSpec(memory_space=pltpu.VMEM)] + [any_spec] * (len(operands) - 1),
        out_specs=any_spec,
        out_shape=jax.ShapeDtypeStruct((wire_rows, 3 * UNIT), jnp.bfloat16),
        input_output_aliases={} if result is None else {4: 0},
        scratch_shapes=[
            pltpu.VMEM((D, FF), jnp.bfloat16),
            pltpu.VMEM((D, FF), jnp.bfloat16),
            pltpu.VMEM((FF, D), jnp.bfloat16),
            pltpu.VMEM((rows, 2 * D), jnp.bfloat16),
            pltpu.VMEM((rows, FF), jnp.bfloat16),
            pltpu.VMEM((rows, FF), jnp.bfloat16),
            pltpu.VMEM((rows, D), jnp.bfloat16),
            pltpu.VMEM((wire_rows, back), jnp.bfloat16),
            pltpu.SemaphoreType.DMA((3, 4)),
            pltpu.SemaphoreType.DMA,
        ],
        compiler_params=pltpu.CompilerParams(vmem_limit_bytes=54 * MIB),
        cost_estimate=pl.CostEstimate(
            flops=2 * rows * 5 * D * FF, bytes_accessed=3 * D * FF * 2, transcendentals=rows * FF
        ),
        name="expert_gradients",
    )(*operands)


def combine_kernel(ids_ref, weight_ref, y_ref, out_ref):
    ids, weight = ids_ref[...], weight_ref[...]
    lanes = iota((TOK, EXPERTS), 1)
    dense = jnp.zeros((TOK, EXPERTS), jnp.float32)
    for k in range(TOP):
        dense = dense + jnp.where(ids[:, k : k + 1] == lanes, weight[:, k : k + 1], 0.0)
    rows = EXPERTS * 8
    spread = one(iota((EXPERTS, rows), 1) // 8 == iota((EXPERTS, rows), 0)).astype(jnp.bfloat16)
    high = dense.astype(jnp.bfloat16)
    low = (dense - high.astype(jnp.float32)).astype(jnp.bfloat16)
    rank = ranked(ids).astype(jnp.bfloat16)
    rank, high, low = (
        jnp.dot(v, spread, preferred_element_type=jnp.float32) for v in (rank, high, low)
    )
    rank = rank.astype(jnp.int32)
    r = iota((TOK, rows), 1) % 8
    both = jnp.concatenate([high, low], axis=0)

    def weights(c, first, a):
        keep = (rank == first + r % c) & (r // c == a)
        keep = jnp.concatenate([keep, keep], axis=0)
        return jnp.where(keep, both, 0.0).astype(jnp.bfloat16)

    for h in range(2):
        four = weights(4, 0, h)
        for half in range(2):
            q = 2 * h + half
            total = jnp.dot(four, y_ref[:, half * UNIT : (half + 1) * UNIT], preferred_element_type=jnp.float32)
            total = total + jnp.dot(
                weights(2, 4, q), y_ref[:, 2 * UNIT : 3 * UNIT], preferred_element_type=jnp.float32
            )
            out_ref[:, q * UNIT : (q + 1) * UNIT] = (total[:TOK] + total[TOK:]).astype(jnp.bfloat16)


def combine(ids, weight, y):
    vmem = pl.BlockSpec(memory_space=pltpu.VMEM)
    return pl.pallas_call(
        combine_kernel,
        in_specs=[vmem] * 3,
        out_specs=vmem,
        out_shape=jax.ShapeDtypeStruct((TOK, D), jnp.bfloat16),
        compiler_params=pltpu.CompilerParams(vmem_limit_bytes=32 * MIB),
        cost_estimate=pl.CostEstimate(
            flops=2 * 2 * TOK * 2 * EXPERTS * 8 * D, bytes_accessed=EXPERTS * 8 * 3 * UNIT * 2, transcendentals=0
        ),
        name="combine_routes",
    )(ids, weight, y)


def exchange(wire):
    blocks = wire.reshape(EXPERTS, 8, wire.shape[1])
    return lax.all_to_all(blocks, AXES, split_axis=0, concat_axis=0, tiled=True).reshape(wire.shape)


def shards(tokens, grad_out, expert_ids, gate_weights, w_gate, w_up, w_down):
    w_gate, w_up, w_down = w_gate[0], w_up[0], w_down[0]
    wires = [exchange(pack(c, first, expert_ids, tokens, grad_out)) for c, first in PARTS]
    result = ffn(4, 0, wires[0], w_gate, w_up, w_down)
    result = ffn(2, 2 * UNIT, wires[1], w_gate, w_up, w_down, result)
    return combine(expert_ids, gate_weights, exchange(result))


def solution(mesh):
    rows = P(AXES, None)
    experts = P(AXES, None, None)
    return jax.shard_map(
        shards,
        mesh=mesh,
        in_specs=(rows, rows, rows, rows, experts, experts, experts),
        out_specs=rows,
        check_vma=False,
    )
```

time: 410 us -> 266 us (0.65)
  blocking collectives: 177 us -> 0 us
  waiting for transfers between devices: 86.6 us -> 163 us
  Pallas kernels: 0 us -> 67.9 us
  local copies, waits for them, and re-layouts: 70.3 us -> 8.03 us
  matrix products: 55.2 us -> 0 us
  starting transfers between devices: 5.67 us -> 25.6 us
  other arithmetic: 13.1 us -> 0 us
    all_to_all x1 -> x0, blocking collectives: 177 us -> none  [shards(): lax.all_to_all(packed, ('node', 'local'), split_axis=0, concat_axis=0, ti...]
    all_to_all x1 -> x3, waiting for transfers between devices: 86.6 us -> 163 us  [exchange(): lax.all_to_all(blocks, AXES, split_axis=0, concat_axis=0, tiled=True)]
    pallas_call x0 -> x5, Pallas kernels: none -> 67.9 us  [the longest x2 50.3 us: ffn(): pl.pallas_call(functools.partial(ffn_kernel, c, out_at), in_specs=[pl.Blo...]
    dot_general x6 -> x0, matrix products: 55.2 us -> none  [the longest x1 12.4 us: expert_rows(): jnp.einsum('erf,edf->erd', up_grad, w_up, preferred_element_type=jnp.floa...]
    another operation x5 -> x0, local copies, waits for them, and re-layouts: 26.2 us -> none  [the longest x1 16.5 us: expert_rows(): jnp.moveaxis(packed, 1, 0)]
    reshape x2 -> x0, local copies, waits for them, and re-layouts: 25.6 us -> none  [the longest x1 15.9 us: shards(): packed.reshape(devices_all, local_experts, capacity, 2 * model_width)]
    all_to_all x1 -> x3, starting transfers between devices: 5.67 us -> 25.6 us  [exchange(): lax.all_to_all(blocks, AXES, split_axis=0, concat_axis=0, tiled=True)]
    gather x1 -> x0, local copies, waits for them, and re-layouts: 17.1 us -> none  [shards(): route_grads = returned[safe_slot]]
  transfers between devices with their start and end apart: 1 -> 3, of which waited for: 1 -> 3; matrix products, arithmetic and copies ran while one was open for 0% -> 0% of each run, Pallas kernels for 0% -> 13%
where the time goes in v1:
time: 266 us; the launch traced here: 265 us
  waiting for transfers between devices  163 us (61%)
  Pallas kernels  67.9 us (26%)
  starting transfers between devices  25.6 us (10%)
  local copies, waits for them, and re-layouts  8.03 us (3%)
    all_to_all x3, waiting for transfers between devices, exchange(): lax.all_to_all(blocks, AXES, split_axis=0, concat_axis=0, tiled=True)  163 us
    pallas_call x2, Pallas kernels, ffn(): pl.pallas_call(functools.partial(ffn_kernel, c, out_at), in_specs=[pl.Blo...  50.3 us
    all_to_all x3, starting transfers between devices, exchange(): lax.all_to_all(blocks, AXES, split_axis=0, concat_axis=0, tiled=True)  25.6 us
    pallas_call x1, Pallas kernels, combine(): pl.pallas_call(combine_kernel, in_specs=[vmem] * 3, out_specs=vmem, out_s...  9 us
    pallas_call x2, Pallas kernels, pack(): pl.pallas_call(functools.partial(pack_kernel, c, first), grid=(c,), in_sp...  8.53 us
    unnamed x16, local copies, waits for them, and re-layouts  8.03 us
  transfers between devices with their start and end apart: 3, of which 3 were waited for; matrix products, arithmetic and copies ran while one was open for 0% of the time, Pallas kernels for 13%

profile of v1, /device:TPU:1, one launch (start us, length us, event | category | flops | bytes accessed | tf_op | source)
XLA Modules:
  0.0 265.0 jit_solution(17598355902873850560)
XLA Ops:
  0.0 0.8 copy.11.ids_ref
  0.8 0.0 copy-start.2
  0.8 1.2 copy-done.2
  2.0 0.0 copy-start.4
  2.0 1.2 copy-done.4
  3.1 4.5 %pack_slots.3 = bf16[1024,3584]{1,0:T(8,128)(2,1)S(1)} custom-call(s32[128,8]{1,0:T(8,128)S(1)} %copy.11.ids_ref, bf16[128,3584]{1,0:T(8,128)(2,1)S(1)} %copy-done.2, bf16[128,3584]{1,0:T(8,128)(2,1)S(1)} %copy-done.4), custom_call_target="tpu_custom_call" | custom-call | flops 1879048192 | bytes 7340032 | tf_op jit(solution)/shard_map/pack_slots/pallas_call | solution.py:71
  7.6 0.0 copy-start
  7.7 3.0 %copy-done = bf16[1024,3584]{1,0:T(8,128)(2,1)} copy-done((bf16[1024,3584]{1,0:T(8,128)(2,1)}, bf16[1024,3584]{1,0:T(8,128)(2,1)S(1)}, u32[]{:S(2)}) %copy-start) | copy-done | bytes 7340056
  10.6 0.0 copy-start.3
  10.7 0.0 copy-start.5
  10.7 11.9 %all-to-all-start.1 = ((bf16[128,8,3584]{2,1,0:T(8,128)(2,1)}), bf16[128,8,3584]{2,1,0:T(8,128)(2,1)}, u32[]{:S(2)}, u32[]{:S(2)}) async-start(bf16[128,8,3584]{2,1,0:T(8,128)(2,1)} %bitcast.9), calls=%async_computation.1 | async-start | bytes 14680064 | tf_op jit(solution)/shard_map/all_to_all | solution.py:254
  22.6 0.0 copy-done.3
  22.6 0.0 copy-done.5
  22.6 4.0 %pack_slots.2 = bf16[1024,1792]{1,0:T(8,128)(2,1)S(1)} custom-call(s32[128,8]{1,0:T(8,128)S(1)} %copy.11.ids_ref, bf16[128,3584]{1,0:T(8,128)(2,1)S(1)} %copy-done.3, bf16[128,3584]{1,0:T(8,128)(2,1)S(1)} %copy-done.3, bf16[128,3584]{1,0:T(8,128)(2,1)S(1)} %copy-done.5, bf16[128,3584]{1,0:T(8,128)(2,1)S(1)} %copy-done.5), custom_call_target="tpu_custom_call" | custom-call | flops 1879048192 | bytes 3670016 | tf_op jit(solution)/shard_map/pack_slots/pallas_call | solution.py:71
  26.6 0.0 copy-start.1
  26.6 1.8 copy-done.1
  28.4 80.9 %all-to-all-done.1 = bf16[128,8,3584]{2,1,0:T(8,128)(2,1)} async-done(((bf16[128,8,3584]{2,1,0:T(8,128)(2,1)}), bf16[128,8,3584]{2,1,0:T(8,128)(2,1)}, u32[]{:S(2)}, u32[]{:S(2)}) %all-to-all-start.1) | async-done | bytes 7340064 | tf_op jit(solution)/shard_map/all_to_all | solution.py:254
  109.3 8.1 %all-to-all-start = ((bf16[128,8,1792]{2,1,0:T(8,128)(2,1)}), bf16[128,8,1792]{2,1,0:T(8,128)(2,1)}, u32[]{:S(2)}, u32[]{:S(2)}) async-start(bf16[128,8,1792]{2,1,0:T(8,128)(2,1)} %bitcast.10), calls=%async_computation | async-start | bytes 7340032 | tf_op jit(solution)/shard_map/all_to_all | solution.py:254
  117.4 31.1 %expert_gradients.2.refs_0_ = bf16[1024,2688]{1,0:T(8,128)(2,1)} custom-call(bf16[1024,3584]{1,0:T(8,128)(2,1)} %bitcast.6.wire_ref, bf16[3584,1024]{1,0:T(8,128)(2,1)} %bitcast.12, bf16[3584,1024]{1,0:T(8,128)(2,1)} %bitcast.14, bf16[1024,3584]{1,0:T(8,128)(2,1)} %bitcast.16), custom_call_target="tpu_custom_call" | custom-call | flops 18790481920 | bytes 22020096 | tf_op jit(solution)/shard_map/expert_gradients/pallas_call | solution.py:177
  148.4 16.1 %all-to-all-done = bf16[128,8,1792]{2,1,0:T(8,128)(2,1)} async-done(((bf16[128,8,1792]{2,1,0:T(8,128)(2,1)}), bf16[128,8,1792]{2,1,0:T(8,128)(2,1)}, u32[]{:S(2)}, u32[]{:S(2)}) %all-to-all-start) | async-done | bytes 3670048 | tf_op jit(solution)/shard_map/all_to_all | solution.py:254
  164.5 19.3 %expert_gradients.3 = bf16[1024,2688]{1,0:T(8,128)(2,1)} custom-call(bf16[1024,1792]{1,0:T(8,128)(2,1)} %bitcast.1.wire_ref, bf16[3584,1024]{1,0:T(8,128)(2,1)} %bitcast.13, bf16[3584,1024]{1,0:T(8,128)(2,1)} %bitcast.15, bf16[1024,3584]{1,0:T(8,128)(2,1)} %bitcast.17, bf16[1024,2688]{1,0:T(8,128)(2,1)} %expert_gradients.2.refs_0_), custom_call_target="tpu_custom_call", output_to_operand_aliasing={{}: (4, {})} | custom-call | flops 9395240960 | bytes 22020096 | tf_op jit(solution)/shard_map/expert_gradients/pallas_call | solution.py:177
  183.8 0.0 copy-start.6
  183.8 5.6 %all-to-all-start.2 = ((bf16[128,8,2688]{2,1,0:T(8,128)(2,1)}), bf16[128,8,2688]{2,1,0:T(8,128)(2,1)}, u32[]{:S(2)}, u32[]{:S(2)}) async-start(bf16[128,8,2688]{2,1,0:T(8,128)(2,1)} %bitcast.11), calls=%async_computation.2 | async-start | bytes 11010048 | tf_op jit(solution)/shard_map/all_to_all | solution.py:254
  189.4 0.0 copy-done.6
  189.4 0.1 copy.12.weight_ref
  189.5 66.5 %all-to-all-done.2 = bf16[128,8,2688]{2,1,0:T(8,128)(2,1)} async-done(((bf16[128,8,2688]{2,1,0:T(8,128)(2,1)}), bf16[128,8,2688]{2,1,0:T(8,128)(2,1)}, u32[]{:S(2)}, u32[]{:S(2)}) %all-to-all-start.2) | async-done | bytes 5505056 | tf_op jit(solution)/shard_map/all_to_all | solution.py:254
  256.0 9.0 %combine_routes.1 = bf16[128,3584]{1,0:T(8,128)(2,1)} custom-call(s32[128,8]{1,0:T(8,128)S(1)} %copy.11.ids_ref, f32[128,8]{1,0:T(8,128)S(1)} %copy.12.weight_ref, bf16[1024,2688]{1,0:T(8,128)(2,1)} %bitcast.8.y_ref), custom_call_target="tpu_custom_call" | custom-call | flops 3758096384 | bytes 5505024 | tf_op jit(solution)/shard_map/combine_routes/pallas_call | solution.py:239
Async XLA Ops:
  0.8 1.2 copy-start.2
  2.0 1.2 copy-start.4
  7.6 3.0 %copy-start = (bf16[1024,3584]{1,0:T(8,128)(2,1)}, bf16[1024,3584]{1,0:T(8,128)(2,1)S(1)}, u32[]{:S(2)}) copy-start(bf16[1024,3584]{1,0:T(8,128)(2,1)S(1)} %pack_slots.3) | copy-start | bytes 22020100
  10.6 11.9 %copy-start.3 = (bf16[128,3584]{1,0:T(8,128)(2,1)S(1)}, bf16[128,3584]{1,0:T(8,128)(2,1)}, u32[]{:S(2)}) copy-start(bf16[128,3584]{1,0:T(8,128)(2,1)} %refs_0_.3) | copy-start | bytes 2752516
  10.7 11.9 %copy-start.5 = (bf16[128,3584]{1,0:T(8,128)(2,1)S(1)}, bf16[128,3584]{1,0:T(8,128)(2,1)}, u32[]{:S(2)}) copy-start(bf16[128,3584]{1,0:T(8,128)(2,1)} %refs_1_.3) | copy-start | bytes 2752516
  10.7 98.6 %all-to-all-start.1 = ((bf16[128,8,3584]{2,1,0:T(8,128)(2,1)}), bf16[128,8,3584]{2,1,0:T(8,128)(2,1)}, u32[]{:S(2)}, u32[]{:S(2)}) async-start(bf16[128,8,3584]{2,1,0:T(8,128)(2,1)} %bitcast.9), calls=%async_computation.1 | async-start | bytes 14680064 | tf_op jit(solution)/shard_map/all_to_all | solution.py:254
  26.6 1.8 copy-start.1
  109.3 55.2 %all-to-all-start = ((bf16[128,8,1792]{2,1,0:T(8,128)(2,1)}), bf16[128,8,1792]{2,1,0:T(8,128)(2,1)}, u32[]{:S(2)}, u32[]{:S(2)}) async-start(bf16[128,8,1792]{2,1,0:T(8,128)(2,1)} %bitcast.10), calls=%async_computation | async-start | bytes 7340032 | tf_op jit(solution)/shard_map/all_to_all | solution.py:254
  183.8 5.6 %copy-start.6 = (f32[128,8]{0,1:T(8,128)S(1)}, f32[128,8]{0,1:T(8,128)}, u32[]{:S(2)}) copy-start(f32[128,8]{0,1:T(8,128)} %param.10) | copy-start | bytes 12292
  183.8 72.2 %all-to-all-start.2 = ((bf16[128,8,2688]{2,1,0:T(8,128)(2,1)}), bf16[128,8,2688]{2,1,0:T(8,128)(2,1)}, u32[]{:S(2)}, u32[]{:S(2)}) async-start(bf16[128,8,2688]{2,1,0:T(8,128)(2,1)} %bitcast.11), calls=%async_computation.2 | async-start | bytes 11010048 | tf_op jit(solution)/shard_map/all_to_all | solution.py:254

commit v2 on v1

v2 whole, which is shorter than its diff:
```python
import functools

import jax
import jax.numpy as jnp
from jax import lax
from jax.experimental import pallas as pl
from jax.experimental.pallas import tpu as pltpu
from jax.sharding import PartitionSpec as P

AXES = ("node", "local")
D = 3584
FF = 1024
TOP = 8
TOK = 128
EXPERTS = 128
UNIT = 896
GROUP = 256
SRC = 32
PACK, PACK2 = 512, 256
MIB = 1 << 20

PARTS = ((4, 0), (2, 4))


def iota(shape, dim):
    return lax.broadcasted_iota(jnp.int32, shape, dim)


def one(mask):
    return jnp.where(mask, 1.0, 0.0)


def routes(ids):
    rows = iota((EXPERTS, TOK), 0)
    chosen = jnp.zeros((EXPERTS, TOK), jnp.float32)
    for k in range(TOP):
        chosen = chosen + one(ids[k : k + 1, :] == rows)
    earlier = one(iota((TOK, TOK), 0) < iota((TOK, TOK), 1))
    rank = jnp.dot(
        chosen.astype(jnp.bfloat16), earlier.astype(jnp.bfloat16), preferred_element_type=jnp.float32
    )
    return jnp.where(chosen > 0.5, rank, 64.0)


def spread_rows(v):
    rows = EXPERTS * 8
    spread = one(iota((rows, EXPERTS), 0) >> 3 == iota((rows, EXPERTS), 1)).astype(jnp.bfloat16)
    return jnp.dot(spread, v.astype(jnp.bfloat16), preferred_element_type=jnp.float32)


def pack_kernel(ids_ref, tokens_hbm, grads_hbm, *refs):
    out_refs, (x, onehot, sems) = refs[: len(PARTS)], refs[len(PARTS) :]

    def loads(i):
        cols = pl.ds(i * PACK, PACK)
        return (
            pltpu.make_async_copy(tokens_hbm.at[:, cols], x.at[pl.ds(0, TOK), cols], sems.at[0, i]),
            pltpu.make_async_copy(grads_hbm.at[:, cols], x.at[pl.ds(TOK, TOK), cols], sems.at[1, i]),
        )

    for i in range(D // PACK):
        for copy in loads(i):
            copy.start()

    rank = spread_rows(routes(ids_ref[...]))
    r = iota((EXPERTS * 8, TOK), 0) & 7

    def hits(c, first):
        slot = (r & (c - 1)).astype(jnp.float32) + first
        chunk = jnp.where(rank == slot, r // c, -1)
        for a in range(8 // c):
            onehot[:, a * TOK : (a + 1) * TOK] = one(chunk == a).astype(jnp.bfloat16)

    (four, first), (two, second) = PARTS
    hits(four, first)
    for i in range(D // PACK):
        for copy in loads(i):
            copy.wait()
        cols = slice(i * PACK, (i + 1) * PACK)
        out_refs[0][:, cols] = jnp.dot(
            onehot[:, : 2 * TOK], x[:, cols], preferred_element_type=jnp.float32
        ).astype(jnp.bfloat16)
    hits(two, second)
    half = D // 2
    for i in range(half // PACK2):
        low, high = slice(i * PACK2, (i + 1) * PACK2), slice(half + i * PACK2, half + (i + 1) * PACK2)
        stack = [x[:TOK, low], x[:TOK, high], x[TOK:, low], x[TOK:, high]]
        out_refs[1][:, low] = jnp.dot(
            onehot[...], jnp.concatenate(stack, axis=0), preferred_element_type=jnp.float32
        ).astype(jnp.bfloat16)


def in_hbm(v):
    return pltpu.with_memory_space_constraint(v, pltpu.HBM)


def pack(ids, tokens, grads):
    rows = EXPERTS * 8
    any_spec, vmem = pl.BlockSpec(memory_space=pl.ANY), pl.BlockSpec(memory_space=pltpu.VMEM)
    return pl.pallas_call(
        pack_kernel,
        in_specs=[vmem, any_spec, any_spec],
        out_specs=[vmem for _ in PARTS],
        out_shape=[jax.ShapeDtypeStruct((rows, c * UNIT), jnp.bfloat16) for c, _ in PARTS],
        scratch_shapes=[
            pltpu.VMEM((2 * TOK, D), jnp.bfloat16),
            pltpu.VMEM((rows, 4 * TOK), jnp.bfloat16),
            pltpu.SemaphoreType.DMA((2, D // PACK)),
        ],
        compiler_params=pltpu.CompilerParams(vmem_limit_bytes=24 * MIB),
        cost_estimate=pl.CostEstimate(
            flops=4 * rows * 2 * TOK * D, bytes_accessed=rows * 6 * UNIT * 2, transcendentals=0
        ),
        name="pack_slots",
    )(ids, in_hbm(tokens), in_hbm(grads))


def sorter(c):
    row, col = iota((GROUP, GROUP), 0), iota((GROUP, GROUP), 1)
    per_chunk = SRC * c
    inner = row % per_chunk
    return one(col == inner // c * 8 + row // per_chunk * c + inner % c).astype(jnp.bfloat16)


def unsorter(c):
    row, col = iota((GROUP, GROUP), 1), iota((GROUP, GROUP), 0)
    per_chunk = SRC * c
    inner = row % per_chunk
    return one(col == inner // c * 8 + row // per_chunk * c + inner % c).astype(jnp.bfloat16)


def ffn_kernel(c, wire_ref, wg_hbm, wu_hbm, wd_hbm, *refs):
    out_hbm, wg, wu, wd, x, up_g, gate_g, res, out, sems, out_sem = refs
    chunks, per_chunk = 8 // c, SRC * c
    width = c * UNIT
    step = 256
    blocks = FF // step

    def loads(j):
        cols = pl.ds(pl.multiple_of(j * step, step), step)
        return (
            pltpu.make_async_copy(wg_hbm.at[:, cols], wg.at[:, cols], sems.at[0, j]),
            pltpu.make_async_copy(wu_hbm.at[:, cols], wu.at[:, cols], sems.at[1, j]),
            pltpu.make_async_copy(wd_hbm.at[cols, :], wd.at[cols, :], sems.at[2, j]),
        )

    for j in range(blocks):
        for copy in loads(j):
            copy.start()

    sort = sorter(c)

    @pl.loop(0, EXPERTS // SRC)
    def _(g):
        rows_in = pl.ds(pl.multiple_of(g * GROUP, GROUP), GROUP)
        rows_x = pl.ds(pl.multiple_of(g * per_chunk, per_chunk), per_chunk)
        for u in range(c):
            part = jnp.dot(
                sort, wire_ref[rows_in, u * UNIT : (u + 1) * UNIT], preferred_element_type=jnp.float32
            ).astype(jnp.bfloat16)
            for a in range(chunks):
                at = a * width + u * UNIT
                x[rows_x, at : at + UNIT] = part[a * per_chunk : (a + 1) * per_chunk]

    @pl.loop(0, blocks)
    def _(j):
        for copy in loads(j):
            copy.wait()
        cols = pl.ds(pl.multiple_of(j * step, step), step)
        gate_pre = jnp.dot(x[:, :D], wg[:, cols], preferred_element_type=jnp.float32)
        up_pre = jnp.dot(x[:, :D], wu[:, cols], preferred_element_type=jnp.float32)
        hidden = lax.dot_general(
            x[:, D:], wd[cols, :], (((1,), (1,)), ((), ())), preferred_element_type=jnp.float32
        )
        s = jax.nn.sigmoid(gate_pre)
        up_g[:, cols] = (hidden * gate_pre * s).astype(jnp.bfloat16)
        gate_g[:, cols] = (hidden * up_pre * s * (1.0 + gate_pre * (1.0 - s))).astype(jnp.bfloat16)

    @pl.loop(0, D // 512)
    def _(j):
        cols = pl.ds(pl.multiple_of(j * 512, 512), 512)
        nt = (((1,), (1,)), ((), ()))
        total = lax.dot_general(gate_g[...], wg[cols, :], nt, preferred_element_type=jnp.float32)
        total = total + lax.dot_general(up_g[...], wu[cols, :], nt, preferred_element_type=jnp.float32)
        res[:, cols] = total.astype(jnp.bfloat16)

    unsort = unsorter(c)
    back = width // 2

    @pl.loop(0, EXPERTS // SRC)
    def _(g):
        rows_out = pl.ds(pl.multiple_of(g * GROUP, GROUP), GROUP)
        rows_x = pl.ds(pl.multiple_of(g * per_chunk, per_chunk), per_chunk)
        stack = jnp.concatenate([res[rows_x, a * back : (a + 1) * back] for a in range(chunks)], axis=0)
        out[rows_out, :] = jnp.dot(unsort, stack, preferred_element_type=jnp.float32).astype(jnp.bfloat16)

    done = pltpu.make_async_copy(out, out_hbm, out_sem)
    done.start()
    done.wait()


def ffn(c, wire, w_gate, w_up, w_down):
    rows, back = EXPERTS * c, c * UNIT // 2
    wire_rows = EXPERTS * 8
    any_spec = pl.BlockSpec(memory_space=pl.ANY)
    return pl.pallas_call(
        functools.partial(ffn_kernel, c),
        in_specs=[pl.BlockSpec(memory_space=pltpu.VMEM)] + [any_spec] * 3,
        out_specs=any_spec,
        out_shape=jax.ShapeDtypeStruct((wire_rows, back), jnp.bfloat16),
        scratch_shapes=[
            pltpu.VMEM((D, FF), jnp.bfloat16),
            pltpu.VMEM((D, FF), jnp.bfloat16),
            pltpu.VMEM((FF, D), jnp.bfloat16),
            pltpu.VMEM((rows, 2 * D), jnp.bfloat16),
            pltpu.VMEM((rows, FF), jnp.bfloat16),
            pltpu.VMEM((rows, FF), jnp.bfloat16),
            pltpu.VMEM((rows, D), jnp.bfloat16),
            pltpu.VMEM((wire_rows, back), jnp.bfloat16),
            pltpu.SemaphoreType.DMA((3, 4)),
            pltpu.SemaphoreType.DMA,
        ],
        compiler_params=pltpu.CompilerParams(vmem_limit_bytes=54 * MIB),
        cost_estimate=pl.CostEstimate(
            flops=2 * rows * 5 * D * FF, bytes_accessed=3 * D * FF * 2, transcendentals=rows * FF
        ),
        name="expert_gradients",
    )(wire, w_gate, w_up, w_down)


def spread_weights(ids, weight, c, first):
    rows = iota((EXPERTS, TOK), 0)
    dense = jnp.zeros((EXPERTS, TOK), jnp.float32)
    for k in range(TOP):
        dense = dense + jnp.where(ids[k : k + 1, :] == rows, weight[k : k + 1, :], 0.0)
    high = dense.astype(jnp.bfloat16).astype(jnp.float32)
    wide = EXPERTS * c
    spread = one(iota((wide, EXPERTS), 0) // c == iota((wide, EXPERTS), 1)).astype(jnp.bfloat16)
    rank, high, low = (
        jnp.dot(spread, v.astype(jnp.bfloat16), preferred_element_type=jnp.float32)
        for v in (routes(ids), high, dense - high)
    )
    hit = rank == (iota((wide, TOK), 0) % c).astype(jnp.float32) + first
    pair = [jnp.where(hit, v, 0.0).T for v in (high, low)]
    return jnp.concatenate(pair, axis=0).astype(jnp.bfloat16)


def slot_rows(c, y_ref, rows_ref):
    sort, per_chunk, back = sorter(c), SRC * c, c * UNIT // 2
    for g in range(EXPERTS // SRC):
        part = jnp.dot(
            sort, y_ref[g * GROUP : (g + 1) * GROUP, :], preferred_element_type=jnp.float32
        ).astype(jnp.bfloat16)
        for a in range(8 // c):
            rows_ref[g * per_chunk : (g + 1) * per_chunk, a * back : (a + 1) * back] = part[
                a * per_chunk : (a + 1) * per_chunk
            ]


def first_combine_kernel(ids_ref, weight_ref, y_ref, sum_ref, late_ref, rows_ref):
    ids, weight = ids_ref[...], weight_ref[...]
    late_ref[...] = spread_weights(ids, weight, *PARTS[1])
    slot_rows(4, y_ref, rows_ref)
    four = spread_weights(ids, weight, *PARTS[0])
    for q in range(4):
        cols = slice(q * UNIT, (q + 1) * UNIT)
        total = jnp.dot(four, rows_ref[:, cols], preferred_element_type=jnp.float32)
        sum_ref[:, cols] = total[:TOK] + total[TOK:]


def last_combine_kernel(late_ref, sum_hbm, y_ref, out_ref, sums, rows_ref, sem):
    copy = pltpu.make_async_copy(sum_hbm, sums, sem)
    copy.start()
    slot_rows(2, y_ref, rows_ref)
    copy.wait()
    for q in range(4):
        cols = slice(q * UNIT, (q + 1) * UNIT)
        total = jnp.dot(late_ref[...], rows_ref[:, cols], preferred_element_type=jnp.float32)
        out_ref[:, cols] = (sums[:, cols] + total[:TOK] + total[TOK:]).astype(jnp.bfloat16)


def first_combine(ids, weight, y):
    vmem = pl.BlockSpec(memory_space=pltpu.VMEM)
    c, late = PARTS[0][0], PARTS[1][0]
    return pl.pallas_call(
        first_combine_kernel,
        in_specs=[vmem] * 3,
        out_specs=(vmem, vmem),
        out_shape=(
            pltpu.HBM((TOK, D), jnp.float32),
            pltpu.VMEM((2 * TOK, EXPERTS * late), jnp.bfloat16),
        ),
        scratch_shapes=[pltpu.VMEM((EXPERTS * c, D), jnp.bfloat16)],
        compiler_params=pltpu.CompilerParams(vmem_limit_bytes=40 * MIB),
        cost_estimate=pl.CostEstimate(
            flops=2 * 2 * TOK * EXPERTS * c * D * 2, bytes_accessed=EXPERTS * c * D * 2, transcendentals=0
        ),
        name="combine_first_slots",
    )(ids, weight, y)


def last_combine(late, sums, y):
    vmem = pl.BlockSpec(memory_space=pltpu.VMEM)
    c = PARTS[1][0]
    return pl.pallas_call(
        last_combine_kernel,
        in_specs=[vmem, pl.BlockSpec(memory_space=pl.ANY), vmem],
        out_specs=vmem,
        out_shape=jax.ShapeDtypeStruct((TOK, D), jnp.bfloat16),
        scratch_shapes=[
            pltpu.VMEM((TOK, D), jnp.float32),
            pltpu.VMEM((EXPERTS * c, D), jnp.bfloat16),
            pltpu.SemaphoreType.DMA,
        ],
        compiler_params=pltpu.CompilerParams(vmem_limit_bytes=20 * MIB),
        cost_estimate=pl.CostEstimate(
            flops=2 * 2 * TOK * EXPERTS * c * D * 2, bytes_accessed=EXPERTS * c * D * 2, transcendentals=0
        ),
        name="combine_last_slots",
    )(late, in_hbm(sums), y)


def exchange(wire):
    blocks = wire.reshape(EXPERTS, 8, wire.shape[1])
    return lax.all_to_all(blocks, AXES, split_axis=0, concat_axis=0, tiled=True).reshape(wire.shape)


def shards(tokens, grad_out, expert_ids, gate_weights, w_gate, w_up, w_down):
    w_gate, w_up, w_down = w_gate[0], w_up[0], w_down[0]
    ids, weights = expert_ids.T, gate_weights.T
    returned = []
    for (c, _), wire in zip(PARTS, pack(ids, tokens, grad_out)):
        returned.append(exchange(ffn(c, exchange(wire), w_gate, w_up, w_down)))
    sums, late = first_combine(ids, weights, returned[0])
    return last_combine(late, sums, returned[1])


def solution(mesh):
    rows = P(AXES, None)
    experts = P(AXES, None, None)
    return jax.shard_map(
        shards,
        mesh=mesh,
        in_specs=(rows, rows, rows, rows, experts, experts, experts),
        out_specs=rows,
        check_vma=False,
    )
```

time: 266 us -> 247 us (0.929)
  blocking collectives: 0 us -> 97.9 us
  waiting for transfers between devices: 163 us -> 66.2 us
  starting transfers between devices: 25.6 us -> 15.3 us
  local copies, waits for them, and re-layouts: 8.03 us -> 0.7 us
    all_to_all x0 -> x1, blocking collectives: none -> 97.9 us  [exchange(): lax.all_to_all(blocks, AXES, split_axis=0, concat_axis=0, tiled=True)]
    all_to_all x3, waiting for transfers between devices: 163 us -> 66.2 us  [exchange(): lax.all_to_all(blocks, AXES, split_axis=0, concat_axis=0, tiled=True)]
    all_to_all x3, starting transfers between devices: 25.6 us -> 15.3 us  [exchange(): lax.all_to_all(blocks, AXES, split_axis=0, concat_axis=0, tiled=True)]
    unnamed x16 -> x8, local copies, waits for them, and re-layouts: 8.03 us -> 0.7 us
  transfers between devices with their start and end apart: 3 -> 3, of which waited for: 3 -> 3; matrix products, arithmetic and copies ran while one was open for 0% -> 0% of each run, Pallas kernels for 13% -> 23%
where the time goes in v2:
time: 247 us
  blocking collectives  97.9 us (40%)
  Pallas kernels  66.5 us (27%)
  waiting for transfers between devices  66.2 us (27%)
  starting transfers between devices  15.3 us (6%)
    all_to_all x1, blocking collectives, exchange(): lax.all_to_all(blocks, AXES, split_axis=0, concat_axis=0, tiled=True)  97.9 us
    all_to_all x3, waiting for transfers between devices, exchange(): lax.all_to_all(blocks, AXES, split_axis=0, concat_axis=0, tiled=True)  66.2 us
    pallas_call x2, Pallas kernels, ffn(): pl.pallas_call(functools.partial(ffn_kernel, c), in_specs=[pl.BlockSpec(m...  50.2 us
    all_to_all x3, starting transfers between devices, exchange(): lax.all_to_all(blocks, AXES, split_axis=0, concat_axis=0, tiled=True)  15.3 us
    pallas_call x1, Pallas kernels, pack(): pl.pallas_call(pack_kernel, in_specs=[vmem, any_spec, any_spec], out_spec...  6.64 us
    pallas_call x1, Pallas kernels, first_combine(): pl.pallas_call(first_combine_kernel, in_specs=[vmem] * 3, out_specs=(vmem...  5.99 us
  transfers between devices with their start and end apart: 3, of which 3 were waited for; matrix products, arithmetic and copies ran while one was open for 0% of the time, Pallas kernels for 23%

profile of v2, /device:TPU:1, one launch (start us, length us, event | category | flops | bytes accessed | tf_op | source)
XLA Modules:
  0.0 246.8 jit_solution(7517066177376359383)
XLA Ops:
  0.0 0.0 copy-start.1
  0.0 0.7 copy-done.1
  0.7 6.6 %pack_slots.1 = (bf16[1024,3584]{1,0:T(8,128)(2,1)S(1)}, bf16[1024,1792]{1,0:T(8,128)(2,1)S(1)}) custom-call(s32[8,128]{1,0:T(8,128)S(1)} %bitcast.16, bf16[128,3584]{1,0:T(8,128)(2,1)} %tokens_hbm.1, bf16[128,3584]{1,0:T(8,128)(2,1)} %grads_hbm.1), custom_call_target="tpu_custom_call" | custom-call | flops 3758096384 | bytes 11010048 | tf_op jit(solution)/shard_map/pack_slots/pallas_call | solution.py:100
  7.3 0.0 copy-start
  7.3 97.9 %all_to_all.20 = bf16[128,8,3584]{2,1,0:T(8,128)(2,1)} all-to-all(bf16[128,8,3584]{2,1,0:T(8,128)(2,1)S(1)} %bitcast.13), channel_id=1, replica_groups=mesh['node'=16,'local'=8] {'node','local'}, dimensions={0} | all-to-all | bytes 14680064 | tf_op jit(solution)/shard_map/all_to_all | solution.py:325
  105.2 0.0 copy-done
  105.2 5.6 %all-to-all-start.2 = ((bf16[128,8,1792]{2,1,0:T(8,128)(2,1)}), bf16[128,8,1792]{2,1,0:T(8,128)(2,1)}, u32[]{:S(2)}, u32[]{:S(2)}) async-start(bf16[128,8,1792]{2,1,0:T(8,128)(2,1)} %bitcast.15), calls=%async_computation.2 | async-start | bytes 7340032 | tf_op jit(solution)/shard_map/all_to_all | solution.py:325
  110.9 31.1 %expert_gradients.2 = bf16[1024,1792]{1,0:T(8,128)(2,1)} custom-call(bf16[1024,3584]{1,0:T(8,128)(2,1)} %bitcast.19, bf16[3584,1024]{1,0:T(8,128)(2,1)} %bitcast.22, bf16[3584,1024]{1,0:T(8,128)(2,1)} %bitcast.24, bf16[1024,3584]{1,0:T(8,128)(2,1)} %bitcast.26), custom_call_target="tpu_custom_call" | custom-call | flops 18790481920 | bytes 22020096 | tf_op jit(solution)/shard_map/expert_gradients/pallas_call | solution.py:206
  142.0 16.2 %all-to-all-done.2 = bf16[128,8,1792]{2,1,0:T(8,128)(2,1)} async-done(((bf16[128,8,1792]{2,1,0:T(8,128)(2,1)}), bf16[128,8,1792]{2,1,0:T(8,128)(2,1)}, u32[]{:S(2)}, u32[]{:S(2)}) %all-to-all-start.2) | async-done | bytes 3670048 | tf_op jit(solution)/shard_map/all_to_all | solution.py:325
  158.2 5.4 %all-to-all-start.1 = ((bf16[128,8,1792]{2,1,0:T(8,128)(2,1)}), bf16[128,8,1792]{2,1,0:T(8,128)(2,1)}, u32[]{:S(2)}, u32[]{:S(2)}) async-start(bf16[128,8,1792]{2,1,0:T(8,128)(2,1)} %bitcast.20), calls=%async_computation.1 | async-start | bytes 7340032 | tf_op jit(solution)/shard_map/all_to_all | solution.py:325
  163.5 19.2 %expert_gradients.3 = bf16[1024,896]{1,0:T(8,128)(2,1)} custom-call(bf16[1024,1792]{1,0:T(8,128)(2,1)} %bitcast.10.wire_ref, bf16[3584,1024]{1,0:T(8,128)(2,1)} %bitcast.23, bf16[3584,1024]{1,0:T(8,128)(2,1)} %bitcast.25, bf16[1024,3584]{1,0:T(8,128)(2,1)} %bitcast.27), custom_call_target="tpu_custom_call" | custom-call | flops 9395240960 | bytes 22020096 | tf_op jit(solution)/shard_map/expert_gradients/pallas_call | solution.py:206
  182.7 0.0 copy-start.2
  182.7 0.0 copy-start.3
  182.7 28.1 %all-to-all-done.1 = bf16[128,8,1792]{2,1,0:T(8,128)(2,1)} async-done(((bf16[128,8,1792]{2,1,0:T(8,128)(2,1)}), bf16[128,8,1792]{2,1,0:T(8,128)(2,1)}, u32[]{:S(2)}, u32[]{:S(2)}) %all-to-all-start.1) | async-done | bytes 3670048 | tf_op jit(solution)/shard_map/all_to_all | solution.py:325
  210.8 4.3 %all-to-all-start.3 = ((bf16[128,8,896]{2,1,0:T(8,128)(2,1)}), bf16[128,8,896]{2,1,0:T(8,128)(2,1)S(1)}, u32[]{:S(2)}, u32[]{:S(2)}) async-start(bf16[128,8,896]{2,1,0:T(8,128)(2,1)} %bitcast.21), calls=%async_computation.3 | async-start | bytes 3670016 | tf_op jit(solution)/shard_map/all_to_all | solution.py:325
  215.1 0.0 copy-done.2
  215.1 0.0 copy-done.3
  215.1 6.0 %combine_first_slots.1 = (f32[128,3584]{1,0:T(8,128)}, bf16[256,256]{1,0:T(8,128)(2,1)S(1)}) custom-call(s32[8,128]{1,0:T(8,128)S(1)} %bitcast.17, f32[8,128]{1,0:T(8,128)S(1)} %bitcast.18, bf16[1024,1792]{1,0:T(8,128)(2,1)} %bitcast.8.y_ref), custom_call_target="tpu_custom_call" | custom-call | flops 1879048192 | bytes 3670016 | tf_op jit(solution)/shard_map/combine_first_slots/pallas_call | solution.py:285
  221.1 21.9 %all-to-all-done.3 = bf16[128,8,896]{2,1,0:T(8,128)(2,1)S(1)} async-done(((bf16[128,8,896]{2,1,0:T(8,128)(2,1)}), bf16[128,8,896]{2,1,0:T(8,128)(2,1)S(1)}, u32[]{:S(2)}, u32[]{:S(2)}) %all-to-all-start.3) | async-done | bytes 1835040 | tf_op jit(solution)/shard_map/all_to_all | solution.py:325
  243.0 3.6 %combine_last_slots.1 = bf16[128,3584]{1,0:T(8,128)(2,1)} custom-call(bf16[256,256]{1,0:T(8,128)(2,1)S(1)} %get-tuple-element.10.late_ref, f32[128,3584]{1,0:T(8,128)} %get-tuple-element.11.sum_hbm, bf16[1024,896]{1,0:T(8,128)(2,1)S(1)} %bitcast.14), custom_call_target="tpu_custom_call" | custom-call | flops 939524096 | bytes 1835008 | tf_op jit(solution)/shard_map/combine_last_slots/pallas_call | solution.py:305
Async XLA Ops:
  0.0 0.7 copy-start.1
  7.3 97.9 %copy-start = (bf16[1024,1792]{1,0:T(8,128)(2,1)}, bf16[1024,1792]{1,0:T(8,128)(2,1)S(1)}, u32[]{:S(2)}) copy-start(bf16[1024,1792]{1,0:T(8,128)(2,1)S(1)} %get-tuple-element.12) | copy-start | bytes 11010052
  105.2 52.9 %all-to-all-start.2 = ((bf16[128,8,1792]{2,1,0:T(8,128)(2,1)}), bf16[128,8,1792]{2,1,0:T(8,128)(2,1)}, u32[]{:S(2)}, u32[]{:S(2)}) async-start(bf16[128,8,1792]{2,1,0:T(8,128)(2,1)} %bitcast.15), calls=%async_computation.2 | async-start | bytes 7340032 | tf_op jit(solution)/shard_map/all_to_all | solution.py:325
  158.2 52.6 %all-to-all-start.1 = ((bf16[128,8,1792]{2,1,0:T(8,128)(2,1)}), bf16[128,8,1792]{2,1,0:T(8,128)(2,1)}, u32[]{:S(2)}, u32[]{:S(2)}) async-start(bf16[128,8,1792]{2,1,0:T(8,128)(2,1)} %bitcast.20), calls=%async_computation.1 | async-start | bytes 7340032 | tf_op jit(solution)/shard_map/all_to_all | solution.py:325
  182.7 32.4 %copy-start.2 = (s32[128,8]{0,1:T(8,128)S(1)}, s32[128,8]{0,1:T(8,128)}, u32[]{:S(2)}) copy-start(s32[128,8]{0,1:T(8,128)} %param.9) | copy-start | bytes 12292
  182.7 32.4 %copy-start.3 = (f32[128,8]{0,1:T(8,128)S(1)}, f32[128,8]{0,1:T(8,128)}, u32[]{:S(2)}) copy-start(f32[128,8]{0,1:T(8,128)} %param.10) | copy-start | bytes 12292
  210.8 32.2 %all-to-all-start.3 = ((bf16[128,8,896]{2,1,0:T(8,128)(2,1)}), bf16[128,8,896]{2,1,0:T(8,128)(2,1)S(1)}, u32[]{:S(2)}, u32[]{:S(2)}) async-start(bf16[128,8,896]{2,1,0:T(8,128)(2,1)} %bitcast.21), calls=%async_computation.3 | async-start | bytes 3670016 | tf_op jit(solution)/shard_map/all_to_all | solution.py:325

commit v3 on v2

--- a/solution.py
+++ b/solution.py
@@ -16,7 +16,6 @@
 UNIT = 896
 GROUP = 256
 SRC = 32
-PACK, PACK2 = 512, 256
 MIB = 1 << 20
 
 PARTS = ((4, 0), (2, 4))
@@ -48,21 +47,20 @@
     return jnp.dot(spread, v.astype(jnp.bfloat16), preferred_element_type=jnp.float32)
 
 
-def pack_kernel(ids_ref, tokens_hbm, grads_hbm, *refs):
-    out_refs, (x, onehot, sems) = refs[: len(PARTS)], refs[len(PARTS) :]
-
-    def loads(i):
-        cols = pl.ds(i * PACK, PACK)
-        return (
-            pltpu.make_async_copy(tokens_hbm.at[:, cols], x.at[pl.ds(0, TOK), cols], sems.at[0, i]),
-            pltpu.make_async_copy(grads_hbm.at[:, cols], x.at[pl.ds(TOK, TOK), cols], sems.at[1, i]),
-        )
-
-    for i in range(D // PACK):
-        for copy in loads(i):
-            copy.start()
-
-    rank = spread_rows(routes(ids_ref[...]))
+def pack_kernel(ids_hbm, tokens_hbm, grads_hbm, *refs):
+    out_refs, (ids, x, onehot, sems) = refs[: len(PARTS)], refs[len(PARTS) :]
+
+    load_ids = pltpu.make_async_copy(ids_hbm, ids, sems.at[2])
+    load_ids.start()
+    loads = (
+        pltpu.make_async_copy(tokens_hbm, x.at[pl.ds(0, TOK), :], sems.at[0]),
+        pltpu.make_async_copy(grads_hbm, x.at[pl.ds(TOK, TOK), :], sems.at[1]),
+    )
+    for copy in loads:
+        copy.start()
+
+    load_ids.wait()
+    rank = spread_rows(routes(ids[...]))
     r = iota((EXPERTS * 8, TOK), 0) & 7
 
     def hits(c, first):
@@ -73,17 +71,23 @@
 
     (four, first), (two, second) = PARTS
     hits(four, first)
-    for i in range(D // PACK):
-        for copy in loads(i):
-            copy.wait()
-        cols = slice(i * PACK, (i + 1) * PACK)
+    for copy in loads:
+        copy.wait()
+    half = D // 2
+
+    @pl.loop(0, 2)
+    def _(i):
+        cols = pl.ds(pl.multiple_of(i * half, half), half)
         out_refs[0][:, cols] = jnp.dot(
             onehot[:, : 2 * TOK], x[:, cols], preferred_element_type=jnp.float32
         ).astype(jnp.bfloat16)
+
     hits(two, second)
-    half = D // 2
-    for i in range(half // PACK2):
-        low, high = slice(i * PACK2, (i + 1) * PACK2), slice(half + i * PACK2, half + (i + 1) * PACK2)
+
+    @pl.loop(0, 2)
+    def _(i):
+        low = pl.ds(pl.multiple_of(i * UNIT, UNIT), UNIT)
+        high = pl.ds(pl.multiple_of(half + i * UNIT, UNIT), UNIT)
         stack = [x[:TOK, low], x[:TOK, high], x[TOK:, low], x[TOK:, high]]
         out_refs[1][:, low] = jnp.dot(
             onehot[...], jnp.concatenate(stack, axis=0), preferred_element_type=jnp.float32
@@ -99,20 +103,21 @@
     any_spec, vmem = pl.BlockSpec(memory_space=pl.ANY), pl.BlockSpec(memory_space=pltpu.VMEM)
     return pl.pallas_call(
         pack_kernel,
-        in_specs=[vmem, any_spec, any_spec],
+        in_specs=[any_spec] * 3,
         out_specs=[vmem for _ in PARTS],
         out_shape=[jax.ShapeDtypeStruct((rows, c * UNIT), jnp.bfloat16) for c, _ in PARTS],
         scratch_shapes=[
+            pltpu.VMEM((TOP, TOK), jnp.int32),
             pltpu.VMEM((2 * TOK, D), jnp.bfloat16),
             pltpu.VMEM((rows, 4 * TOK), jnp.bfloat16),
-            pltpu.SemaphoreType.DMA((2, D // PACK)),
+            pltpu.SemaphoreType.DMA((3,)),
         ],
         compiler_params=pltpu.CompilerParams(vmem_limit_bytes=24 * MIB),
         cost_estimate=pl.CostEstimate(
             flops=4 * rows * 2 * TOK * D, bytes_accessed=rows * 6 * UNIT * 2, transcendentals=0
         ),
         name="pack_slots",
-    )(ids, in_hbm(tokens), in_hbm(grads))
+    )(in_hbm(ids), in_hbm(tokens), in_hbm(grads))
 
 
 def sorter(c):

time: 247 us -> 247 us (level)
  no operation moved by 1% of the time
where the time goes in v3:
time: 247 us; the launch traced here: 246 us
  blocking collectives  97.9 us (40%)
  Pallas kernels  66.5 us (27%)
  waiting for transfers between devices  66.2 us (27%)
  starting transfers between devices  15.5 us (6%)
    all_to_all x1, blocking collectives, exchange(): lax.all_to_all(blocks, AXES, split_axis=0, concat_axis=0, tiled=True)  97.9 us
    all_to_all x3, waiting for transfers between devices, exchange(): lax.all_to_all(blocks, AXES, split_axis=0, concat_axis=0, tiled=True)  66.2 us
    pallas_call x2, Pallas kernels, ffn(): pl.pallas_call(functools.partial(ffn_kernel, c), in_specs=[pl.BlockSpec(m...  50.2 us
    all_to_all x3, starting transfers between devices, exchange(): lax.all_to_all(blocks, AXES, split_axis=0, concat_axis=0, tiled=True)  15.5 us
    pallas_call x1, Pallas kernels, pack(): pl.pallas_call(pack_kernel, in_specs=[any_spec] * 3, out_specs=[vmem for...  6.65 us
    pallas_call x1, Pallas kernels, first_combine(): pl.pallas_call(first_combine_kernel, in_specs=[vmem] * 3, out_specs=(vmem...  6 us
  transfers between devices with their start and end apart: 3, of which 3 were waited for; matrix products, arithmetic and copies ran while one was open for 0% of the time, Pallas kernels for 23%

profile of v3, /device:TPU:1, one launch (start us, length us, event | category | flops | bytes accessed | tf_op | source)
XLA Modules:
  0.0 246.3 jit_solution(7626771400554639243)
XLA Ops:
  0.0 6.6 %pack_slots.1 = (bf16[1024,3584]{1,0:T(8,128)(2,1)S(1)}, bf16[1024,1792]{1,0:T(8,128)(2,1)S(1)}) custom-call(s32[8,128]{1,0:T(8,128)} %bitcast.16, bf16[128,3584]{1,0:T(8,128)(2,1)} %tokens_hbm.1, bf16[128,3584]{1,0:T(8,128)(2,1)} %grads_hbm.1), custom_call_target="tpu_custom_call" | custom-call | flops 3758096384 | bytes 11010048 | tf_op jit(solution)/shard_map/pack_slots/pallas_call | solution.py:104
  6.7 0.0 copy-start
  6.7 97.9 %all_to_all.20 = bf16[128,8,3584]{2,1,0:T(8,128)(2,1)} all-to-all(bf16[128,8,3584]{2,1,0:T(8,128)(2,1)S(1)} %bitcast.13), channel_id=1, replica_groups=mesh['node'=16,'local'=8] {'node','local'}, dimensions={0} | all-to-all | bytes 14680064 | tf_op jit(solution)/shard_map/all_to_all | solution.py:330
  104.5 0.0 copy-done
  104.5 5.7 %all-to-all-start.2 = ((bf16[128,8,1792]{2,1,0:T(8,128)(2,1)}), bf16[128,8,1792]{2,1,0:T(8,128)(2,1)}, u32[]{:S(2)}, u32[]{:S(2)}) async-start(bf16[128,8,1792]{2,1,0:T(8,128)(2,1)} %bitcast.15), calls=%async_computation.2 | async-start | bytes 7340032 | tf_op jit(solution)/shard_map/all_to_all | solution.py:330
  110.2 31.1 %expert_gradients.2 = bf16[1024,1792]{1,0:T(8,128)(2,1)} custom-call(bf16[1024,3584]{1,0:T(8,128)(2,1)} %bitcast.19, bf16[3584,1024]{1,0:T(8,128)(2,1)} %bitcast.22, bf16[3584,1024]{1,0:T(8,128)(2,1)} %bitcast.24, bf16[1024,3584]{1,0:T(8,128)(2,1)} %bitcast.26), custom_call_target="tpu_custom_call" | custom-call | flops 18790481920 | bytes 22020096 | tf_op jit(solution)/shard_map/expert_gradients/pallas_call | solution.py:211
  141.3 16.2 %all-to-all-done.2 = bf16[128,8,1792]{2,1,0:T(8,128)(2,1)} async-done(((bf16[128,8,1792]{2,1,0:T(8,128)(2,1)}), bf16[128,8,1792]{2,1,0:T(8,128)(2,1)}, u32[]{:S(2)}, u32[]{:S(2)}) %all-to-all-start.2) | async-done | bytes 3670048 | tf_op jit(solution)/shard_map/all_to_all | solution.py:330
  157.5 5.4 %all-to-all-start.1 = ((bf16[128,8,1792]{2,1,0:T(8,128)(2,1)}), bf16[128,8,1792]{2,1,0:T(8,128)(2,1)}, u32[]{:S(2)}, u32[]{:S(2)}) async-start(bf16[128,8,1792]{2,1,0:T(8,128)(2,1)} %bitcast.20), calls=%async_computation.1 | async-start | bytes 7340032 | tf_op jit(solution)/shard_map/all_to_all | solution.py:330
  162.8 19.2 %expert_gradients.3 = bf16[1024,896]{1,0:T(8,128)(2,1)} custom-call(bf16[1024,1792]{1,0:T(8,128)(2,1)} %bitcast.10.wire_ref, bf16[3584,1024]{1,0:T(8,128)(2,1)} %bitcast.23, bf16[3584,1024]{1,0:T(8,128)(2,1)} %bitcast.25, bf16[1024,3584]{1,0:T(8,128)(2,1)} %bitcast.27), custom_call_target="tpu_custom_call" | custom-call | flops 9395240960 | bytes 22020096 | tf_op jit(solution)/shard_map/expert_gradients/pallas_call | solution.py:211
  182.0 0.0 copy-start.1
  182.0 0.0 copy-start.2
  182.0 28.1 %all-to-all-done.1 = bf16[128,8,1792]{2,1,0:T(8,128)(2,1)} async-done(((bf16[128,8,1792]{2,1,0:T(8,128)(2,1)}), bf16[128,8,1792]{2,1,0:T(8,128)(2,1)}, u32[]{:S(2)}, u32[]{:S(2)}) %all-to-all-start.1) | async-done | bytes 3670048 | tf_op jit(solution)/shard_map/all_to_all | solution.py:330
  210.1 4.5 %all-to-all-start.3 = ((bf16[128,8,896]{2,1,0:T(8,128)(2,1)}), bf16[128,8,896]{2,1,0:T(8,128)(2,1)S(1)}, u32[]{:S(2)}, u32[]{:S(2)}) async-start(bf16[128,8,896]{2,1,0:T(8,128)(2,1)} %bitcast.21), calls=%async_computation.3 | async-start | bytes 3670016 | tf_op jit(solution)/shard_map/all_to_all | solution.py:330
  214.6 0.0 copy-done.1
  214.6 0.0 copy-done.2
  214.6 6.0 %combine_first_slots.1 = (f32[128,3584]{1,0:T(8,128)}, bf16[256,256]{1,0:T(8,128)(2,1)S(1)}) custom-call(s32[8,128]{1,0:T(8,128)S(1)} %bitcast.17, f32[8,128]{1,0:T(8,128)S(1)} %bitcast.18, bf16[1024,1792]{1,0:T(8,128)(2,1)} %bitcast.8.y_ref), custom_call_target="tpu_custom_call" | custom-call | flops 1879048192 | bytes 3670016 | tf_op jit(solution)/shard_map/combine_first_slots/pallas_call | solution.py:290
  220.6 21.9 %all-to-all-done.3 = bf16[128,8,896]{2,1,0:T(8,128)(2,1)S(1)} async-done(((bf16[128,8,896]{2,1,0:T(8,128)(2,1)}), bf16[128,8,896]{2,1,0:T(8,128)(2,1)S(1)}, u32[]{:S(2)}, u32[]{:S(2)}) %all-to-all-start.3) | async-done | bytes 1835040 | tf_op jit(solution)/shard_map/all_to_all | solution.py:330
  242.5 3.6 %combine_last_slots.1 = bf16[128,3584]{1,0:T(8,128)(2,1)} custom-call(bf16[256,256]{1,0:T(8,128)(2,1)S(1)} %get-tuple-element.10.late_ref, f32[128,3584]{1,0:T(8,128)} %get-tuple-element.11.sum_hbm, bf16[1024,896]{1,0:T(8,128)(2,1)S(1)} %bitcast.14), custom_call_target="tpu_custom_call" | custom-call | flops 939524096 | bytes 1835008 | tf_op jit(solution)/shard_map/combine_last_slots/pallas_call | solution.py:310
Async XLA Ops:
  6.7 97.9 %copy-start = (bf16[1024,1792]{1,0:T(8,128)(2,1)}, bf16[1024,1792]{1,0:T(8,128)(2,1)S(1)}, u32[]{:S(2)}) copy-start(bf16[1024,1792]{1,0:T(8,128)(2,1)S(1)} %get-tuple-element.12) | copy-start | bytes 11010052
  104.5 52.9 %all-to-all-start.2 = ((bf16[128,8,1792]{2,1,0:T(8,128)(2,1)}), bf16[128,8,1792]{2,1,0:T(8,128)(2,1)}, u32[]{:S(2)}, u32[]{:S(2)}) async-start(bf16[128,8,1792]{2,1,0:T(8,128)(2,1)} %bitcast.15), calls=%async_computation.2 | async-start | bytes 7340032 | tf_op jit(solution)/shard_map/all_to_all | solution.py:330
  157.5 52.6 %all-to-all-start.1 = ((bf16[128,8,1792]{2,1,0:T(8,128)(2,1)}), bf16[128,8,1792]{2,1,0:T(8,128)(2,1)}, u32[]{:S(2)}, u32[]{:S(2)}) async-start(bf16[128,8,1792]{2,1,0:T(8,128)(2,1)} %bitcast.20), calls=%async_computation.1 | async-start | bytes 7340032 | tf_op jit(solution)/shard_map/all_to_all | solution.py:330
  182.0 32.6 %copy-start.1 = (s32[128,8]{0,1:T(8,128)S(1)}, s32[128,8]{0,1:T(8,128)}, u32[]{:S(2)}) copy-start(s32[128,8]{0,1:T(8,128)} %param.9) | copy-start | bytes 12292
  182.0 32.6 %copy-start.2 = (f32[128,8]{0,1:T(8,128)S(1)}, f32[128,8]{0,1:T(8,128)}, u32[]{:S(2)}) copy-start(f32[128,8]{0,1:T(8,128)} %param.10) | copy-start | bytes 12292
  210.1 32.4 %all-to-all-start.3 = ((bf16[128,8,896]{2,1,0:T(8,128)(2,1)}), bf16[128,8,896]{2,1,0:T(8,128)(2,1)S(1)}, u32[]{:S(2)}, u32[]{:S(2)}) async-start(bf16[128,8,896]{2,1,0:T(8,128)(2,1)} %bitcast.21), calls=%async_computation.3 | async-start | bytes 3670016 | tf_op jit(solution)/shard_map/all_to_all | solution.py:330

commit v4 on v3

--- a/solution.py
+++ b/solution.py
@@ -15,6 +15,7 @@
 EXPERTS = 128
 UNIT = 896
 GROUP = 256
+BLOCK = 512
 SRC = 32
 MIB = 1 << 20
 
@@ -41,14 +42,8 @@
     return jnp.where(chosen > 0.5, rank, 64.0)
 
 
-def spread_rows(v):
-    rows = EXPERTS * 8
-    spread = one(iota((rows, EXPERTS), 0) >> 3 == iota((rows, EXPERTS), 1)).astype(jnp.bfloat16)
-    return jnp.dot(spread, v.astype(jnp.bfloat16), preferred_element_type=jnp.float32)
-
-
 def pack_kernel(ids_hbm, tokens_hbm, grads_hbm, *refs):
-    out_refs, (ids, x, onehot, sems) = refs[: len(PARTS)], refs[len(PARTS) :]
+    out_refs, (ids, x, sems) = refs[: len(PARTS)], refs[len(PARTS) :]
 
     load_ids = pltpu.make_async_copy(ids_hbm, ids, sems.at[2])
     load_ids.start()
@@ -60,38 +55,32 @@
         copy.start()
 
     load_ids.wait()
-    rank = spread_rows(routes(ids[...]))
-    r = iota((EXPERTS * 8, TOK), 0) & 7
-
-    def hits(c, first):
+    ranks = routes(ids[...]).astype(jnp.bfloat16)
+    spread = one(iota((BLOCK, BLOCK // 8), 0) >> 3 == iota((BLOCK, BLOCK // 8), 1)).astype(jnp.bfloat16)
+    r = iota((BLOCK, TOK), 0) & 7
+    blocks = EXPERTS * 8 // BLOCK
+
+    def onehot(g, c, first):
+        rank = ranks[g * BLOCK // 8 : (g + 1) * BLOCK // 8, :]
+        rank = jnp.dot(spread, rank, preferred_element_type=jnp.float32)
         slot = (r & (c - 1)).astype(jnp.float32) + first
         chunk = jnp.where(rank == slot, r // c, -1)
-        for a in range(8 // c):
-            onehot[:, a * TOK : (a + 1) * TOK] = one(chunk == a).astype(jnp.bfloat16)
-
-    (four, first), (two, second) = PARTS
-    hits(four, first)
+        return jnp.concatenate([one(chunk == a).astype(jnp.bfloat16) for a in range(8 // c)], axis=1)
+
+    def store(out_ref, g, hits, rows):
+        out_ref[g * BLOCK : (g + 1) * BLOCK, :] = jnp.dot(
+            hits, rows, preferred_element_type=jnp.float32
+        ).astype(jnp.bfloat16)
+
+    hits = onehot(0, *PARTS[0])
     for copy in loads:
         copy.wait()
+    for g in range(blocks):
+        store(out_refs[0], g, hits if g == 0 else onehot(g, *PARTS[0]), x[...])
     half = D // 2
-
-    @pl.loop(0, 2)
-    def _(i):
-        cols = pl.ds(pl.multiple_of(i * half, half), half)
-        out_refs[0][:, cols] = jnp.dot(
-            onehot[:, : 2 * TOK], x[:, cols], preferred_element_type=jnp.float32
-        ).astype(jnp.bfloat16)
-
-    hits(two, second)
-
-    @pl.loop(0, 2)
-    def _(i):
-        low = pl.ds(pl.multiple_of(i * UNIT, UNIT), UNIT)
-        high = pl.ds(pl.multiple_of(half + i * UNIT, UNIT), UNIT)
-        stack = [x[:TOK, low], x[:TOK, high], x[TOK:, low], x[TOK:, high]]
-        out_refs[1][:, low] = jnp.dot(
-            onehot[...], jnp.concatenate(stack, axis=0), preferred_element_type=jnp.float32
-        ).astype(jnp.bfloat16)
+    for g in range(blocks):
+        stack = [x[:TOK, :half], x[:TOK, half:], x[TOK:, :half], x[TOK:, half:]]
+        store(out_refs[1], g, onehot(g, *PARTS[1]), jnp.concatenate(stack, axis=0))
 
 
 def in_hbm(v):
@@ -109,7 +98,6 @@
         scratch_shapes=[
             pltpu.VMEM((TOP, TOK), jnp.int32),
             pltpu.VMEM((2 * TOK, D), jnp.bfloat16),
-            pltpu.VMEM((rows, 4 * TOK), jnp.bfloat16),
             pltpu.SemaphoreType.DMA((3,)),
         ],
         compiler_params=pltpu.CompilerParams(vmem_limit_bytes=24 * MIB),
@@ -278,10 +266,8 @@
     copy.start()
     slot_rows(2, y_ref, rows_ref)
     copy.wait()
-    for q in range(4):
-        cols = slice(q * UNIT, (q + 1) * UNIT)
-        total = jnp.dot(late_ref[...], rows_ref[:, cols], preferred_element_type=jnp.float32)
-        out_ref[:, cols] = (sums[:, cols] + total[:TOK] + total[TOK:]).astype(jnp.bfloat16)
+    total = jnp.dot(late_ref[...], rows_ref[...], preferred_element_type=jnp.float32)
+    out_ref[...] = (sums[...] + total[:TOK] + total[TOK:]).astype(jnp.bfloat16)
 
 
 def first_combine(ids, weight, y):

time: 247 us -> 246 us (level)
  no operation moved by 1% of the time
where the time goes in v4:
time: 246 us; the launch traced here: 245 us
  blocking collectives  97.9 us (40%)
  waiting for transfers between devices  66.2 us (27%)
  Pallas kernels  65.5 us (27%)
  starting transfers between devices  15.3 us (6%)
    all_to_all x1, blocking collectives, exchange(): lax.all_to_all(blocks, AXES, split_axis=0, concat_axis=0, tiled=True)  97.9 us
    all_to_all x3, waiting for transfers between devices, exchange(): lax.all_to_all(blocks, AXES, split_axis=0, concat_axis=0, tiled=True)  66.2 us
    pallas_call x2, Pallas kernels, ffn(): pl.pallas_call(functools.partial(ffn_kernel, c), in_specs=[pl.BlockSpec(m...  50.2 us
    all_to_all x3, starting transfers between devices, exchange(): lax.all_to_all(blocks, AXES, split_axis=0, concat_axis=0, tiled=True)  15.3 us
    pallas_call x1, Pallas kernels, first_combine(): pl.pallas_call(first_combine_kernel, in_specs=[vmem] * 3, out_specs=(vmem...  6 us
    pallas_call x1, Pallas kernels, pack(): pl.pallas_call(pack_kernel, in_specs=[any_spec] * 3, out_specs=[vmem for...  5.74 us
  transfers between devices with their start and end apart: 3, of which 3 were waited for; matrix products, arithmetic and copies ran while one was open for 0% of the time, Pallas kernels for 23%

profile of v4, /device:TPU:1, one launch (start us, length us, event | category | flops | bytes accessed | tf_op | source)
XLA Modules:
  0.0 245.2 jit_solution(3342014554399096498)
XLA Ops:
  0.0 5.7 %pack_slots.1 = (bf16[1024,3584]{1,0:T(8,128)(2,1)S(1)}, bf16[1024,1792]{1,0:T(8,128)(2,1)S(1)}) custom-call(s32[8,128]{1,0:T(8,128)} %bitcast.16, bf16[128,3584]{1,0:T(8,128)(2,1)} %tokens_hbm.1, bf16[128,3584]{1,0:T(8,128)(2,1)} %grads_hbm.1), custom_call_target="tpu_custom_call" | custom-call | flops 3758096384 | bytes 11010048 | tf_op jit(solution)/shard_map/pack_slots/pallas_call | solution.py:93
  5.8 0.0 copy-start
  5.8 97.9 %all_to_all.20 = bf16[128,8,3584]{2,1,0:T(8,128)(2,1)} all-to-all(bf16[128,8,3584]{2,1,0:T(8,128)(2,1)S(1)} %bitcast.13), channel_id=1, replica_groups=mesh['node'=16,'local'=8] {'node','local'}, dimensions={0} | all-to-all | bytes 14680064 | tf_op jit(solution)/shard_map/all_to_all | solution.py:316
  103.6 0.0 copy-done
  103.6 5.7 %all-to-all-start.2 = ((bf16[128,8,1792]{2,1,0:T(8,128)(2,1)}), bf16[128,8,1792]{2,1,0:T(8,128)(2,1)}, u32[]{:S(2)}, u32[]{:S(2)}) async-start(bf16[128,8,1792]{2,1,0:T(8,128)(2,1)} %bitcast.15), calls=%async_computation.2 | async-start | bytes 7340032 | tf_op jit(solution)/shard_map/all_to_all | solution.py:316
  109.3 31.1 %expert_gradients.2 = bf16[1024,1792]{1,0:T(8,128)(2,1)} custom-call(bf16[1024,3584]{1,0:T(8,128)(2,1)} %bitcast.19, bf16[3584,1024]{1,0:T(8,128)(2,1)} %bitcast.22, bf16[3584,1024]{1,0:T(8,128)(2,1)} %bitcast.24, bf16[1024,3584]{1,0:T(8,128)(2,1)} %bitcast.26), custom_call_target="tpu_custom_call" | custom-call | flops 18790481920 | bytes 22020096 | tf_op jit(solution)/shard_map/expert_gradients/pallas_call | solution.py:199
  140.4 16.2 %all-to-all-done.2 = bf16[128,8,1792]{2,1,0:T(8,128)(2,1)} async-done(((bf16[128,8,1792]{2,1,0:T(8,128)(2,1)}), bf16[128,8,1792]{2,1,0:T(8,128)(2,1)}, u32[]{:S(2)}, u32[]{:S(2)}) %all-to-all-start.2) | async-done | bytes 3670048 | tf_op jit(solution)/shard_map/all_to_all | solution.py:316
  156.6 5.4 %all-to-all-start.1 = ((bf16[128,8,1792]{2,1,0:T(8,128)(2,1)}), bf16[128,8,1792]{2,1,0:T(8,128)(2,1)}, u32[]{:S(2)}, u32[]{:S(2)}) async-start(bf16[128,8,1792]{2,1,0:T(8,128)(2,1)} %bitcast.20), calls=%async_computation.1 | async-start | bytes 7340032 | tf_op jit(solution)/shard_map/all_to_all | solution.py:316
  162.0 19.2 %expert_gradients.3 = bf16[1024,896]{1,0:T(8,128)(2,1)} custom-call(bf16[1024,1792]{1,0:T(8,128)(2,1)} %bitcast.10.wire_ref, bf16[3584,1024]{1,0:T(8,128)(2,1)} %bitcast.23, bf16[3584,1024]{1,0:T(8,128)(2,1)} %bitcast.25, bf16[1024,3584]{1,0:T(8,128)(2,1)} %bitcast.27), custom_call_target="tpu_custom_call" | custom-call | flops 9395240960 | bytes 22020096 | tf_op jit(solution)/shard_map/expert_gradients/pallas_call | solution.py:199
  181.1 0.0 copy-start.1
  181.1 0.0 copy-start.2
  181.1 28.1 %all-to-all-done.1 = bf16[128,8,1792]{2,1,0:T(8,128)(2,1)} async-done(((bf16[128,8,1792]{2,1,0:T(8,128)(2,1)}), bf16[128,8,1792]{2,1,0:T(8,128)(2,1)}, u32[]{:S(2)}, u32[]{:S(2)}) %all-to-all-start.1) | async-done | bytes 3670048 | tf_op jit(solution)/shard_map/all_to_all | solution.py:316
  209.2 4.3 %all-to-all-start.3 = ((bf16[128,8,896]{2,1,0:T(8,128)(2,1)}), bf16[128,8,896]{2,1,0:T(8,128)(2,1)S(1)}, u32[]{:S(2)}, u32[]{:S(2)}) async-start(bf16[128,8,896]{2,1,0:T(8,128)(2,1)} %bitcast.21), calls=%async_computation.3 | async-start | bytes 3670016 | tf_op jit(solution)/shard_map/all_to_all | solution.py:316
  213.5 0.0 copy-done.1
  213.5 0.0 copy-done.2
  213.6 6.0 %combine_first_slots.1 = (f32[128,3584]{1,0:T(8,128)}, bf16[256,256]{1,0:T(8,128)(2,1)S(1)}) custom-call(s32[8,128]{1,0:T(8,128)S(1)} %bitcast.17, f32[8,128]{1,0:T(8,128)S(1)} %bitcast.18, bf16[1024,1792]{1,0:T(8,128)(2,1)} %bitcast.8.y_ref), custom_call_target="tpu_custom_call" | custom-call | flops 1879048192 | bytes 3670016 | tf_op jit(solution)/shard_map/combine_first_slots/pallas_call | solution.py:276
  219.6 21.9 %all-to-all-done.3 = bf16[128,8,896]{2,1,0:T(8,128)(2,1)S(1)} async-done(((bf16[128,8,896]{2,1,0:T(8,128)(2,1)}), bf16[128,8,896]{2,1,0:T(8,128)(2,1)S(1)}, u32[]{:S(2)}, u32[]{:S(2)}) %all-to-all-start.3) | async-done | bytes 1835040 | tf_op jit(solution)/shard_map/all_to_all | solution.py:316
  241.4 3.6 %combine_last_slots.1 = bf16[128,3584]{1,0:T(8,128)(2,1)} custom-call(bf16[256,256]{1,0:T(8,128)(2,1)S(1)} %get-tuple-element.10.late_ref, f32[128,3584]{1,0:T(8,128)} %get-tuple-element.11.sum_hbm, bf16[1024,896]{1,0:T(8,128)(2,1)S(1)} %bitcast.14), custom_call_target="tpu_custom_call" | custom-call | flops 939524096 | bytes 1835008 | tf_op jit(solution)/shard_map/combine_last_slots/pallas_call | solution.py:296
Async XLA Ops:
  5.8 97.9 %copy-start = (bf16[1024,1792]{1,0:T(8,128)(2,1)}, bf16[1024,1792]{1,0:T(8,128)(2,1)S(1)}, u32[]{:S(2)}) copy-start(bf16[1024,1792]{1,0:T(8,128)(2,1)S(1)} %get-tuple-element.12) | copy-start | bytes 11010052
  103.6 52.9 %all-to-all-start.2 = ((bf16[128,8,1792]{2,1,0:T(8,128)(2,1)}), bf16[128,8,1792]{2,1,0:T(8,128)(2,1)}, u32[]{:S(2)}, u32[]{:S(2)}) async-start(bf16[128,8,1792]{2,1,0:T(8,128)(2,1)} %bitcast.15), calls=%async_computation.2 | async-start | bytes 7340032 | tf_op jit(solution)/shard_map/all_to_all | solution.py:316
  156.6 52.6 %all-to-all-start.1 = ((bf16[128,8,1792]{2,1,0:T(8,128)(2,1)}), bf16[128,8,1792]{2,1,0:T(8,128)(2,1)}, u32[]{:S(2)}, u32[]{:S(2)}) async-start(bf16[128,8,1792]{2,1,0:T(8,128)(2,1)} %bitcast.20), calls=%async_computation.1 | async-start | bytes 7340032 | tf_op jit(solution)/shard_map/all_to_all | solution.py:316
  181.1 32.4 %copy-start.1 = (s32[128,8]{0,1:T(8,128)S(1)}, s32[128,8]{0,1:T(8,128)}, u32[]{:S(2)}) copy-start(s32[128,8]{0,1:T(8,128)} %param.9) | copy-start | bytes 12292
  181.1 32.4 %copy-start.2 = (f32[128,8]{0,1:T(8,128)S(1)}, f32[128,8]{0,1:T(8,128)}, u32[]{:S(2)}) copy-start(f32[128,8]{0,1:T(8,128)} %param.10) | copy-start | bytes 12292
  209.2 32.2 %all-to-all-start.3 = ((bf16[128,8,896]{2,1,0:T(8,128)(2,1)}), bf16[128,8,896]{2,1,0:T(8,128)(2,1)S(1)}, u32[]{:S(2)}, u32[]{:S(2)}) async-start(bf16[128,8,896]{2,1,0:T(8,128)(2,1)} %bitcast.21), calls=%async_computation.3 | async-start | bytes 3670016 | tf_op jit(solution)/shard_map/all_to_all | solution.py:316

commit v5 on v4

--- a/solution.py
+++ b/solution.py
@@ -261,13 +261,26 @@
         sum_ref[:, cols] = total[:TOK] + total[TOK:]
 
 
-def last_combine_kernel(late_ref, sum_hbm, y_ref, out_ref, sums, rows_ref, sem):
-    copy = pltpu.make_async_copy(sum_hbm, sums, sem)
-    copy.start()
-    slot_rows(2, y_ref, rows_ref)
-    copy.wait()
-    total = jnp.dot(late_ref[...], rows_ref[...], preferred_element_type=jnp.float32)
-    out_ref[...] = (sums[...] + total[:TOK] + total[TOK:]).astype(jnp.bfloat16)
+def last_combine_kernel(late_hbm, sum_hbm, y_ref, out_hbm, late, sums, rows_ref, out, sems):
+    halves = [pl.ds(h * D // 2, D // 2) for h in range(2)]
+    load_late = pltpu.make_async_copy(late_hbm, late, sems.at[0])
+    loads = [
+        pltpu.make_async_copy(sum_hbm.at[:, cols], sums.at[:, cols], sems.at[1 + h])
+        for h, cols in enumerate(halves)
+    ]
+    for copy in (load_late, *loads):
+        copy.start()
+    slot_rows(PARTS[1][0], y_ref, rows_ref)
+    load_late.wait()
+    stores = []
+    for h, cols in enumerate(halves):
+        total = jnp.dot(late[...], rows_ref[:, cols], preferred_element_type=jnp.float32)
+        loads[h].wait()
+        out[:, cols] = (sums[:, cols] + total[:TOK] + total[TOK:]).astype(jnp.bfloat16)
+        stores.append(pltpu.make_async_copy(out.at[:, cols], out_hbm.at[:, cols], sems.at[3 + h]))
+        stores[-1].start()
+    for copy in stores:
+        copy.wait()
 
 
 def first_combine(ids, weight, y):
@@ -279,7 +292,7 @@
         out_specs=(vmem, vmem),
         out_shape=(
             pltpu.HBM((TOK, D), jnp.float32),
-            pltpu.VMEM((2 * TOK, EXPERTS * late), jnp.bfloat16),
+            pltpu.HBM((2 * TOK, EXPERTS * late), jnp.bfloat16),
         ),
         scratch_shapes=[pltpu.VMEM((EXPERTS * c, D), jnp.bfloat16)],
         compiler_params=pltpu.CompilerParams(vmem_limit_bytes=40 * MIB),
@@ -291,24 +304,26 @@
 
 
 def last_combine(late, sums, y):
-    vmem = pl.BlockSpec(memory_space=pltpu.VMEM)
+    any_spec, vmem = pl.BlockSpec(memory_space=pl.ANY), pl.BlockSpec(memory_space=pltpu.VMEM)
     c = PARTS[1][0]
     return pl.pallas_call(
         last_combine_kernel,
-        in_specs=[vmem, pl.BlockSpec(memory_space=pl.ANY), vmem],
-        out_specs=vmem,
+        in_specs=[any_spec, any_spec, vmem],
+        out_specs=any_spec,
         out_shape=jax.ShapeDtypeStruct((TOK, D), jnp.bfloat16),
         scratch_shapes=[
+            pltpu.VMEM((2 * TOK, EXPERTS * c), jnp.bfloat16),
             pltpu.VMEM((TOK, D), jnp.float32),
             pltpu.VMEM((EXPERTS * c, D), jnp.bfloat16),
-            pltpu.SemaphoreType.DMA,
+            pltpu.VMEM((TOK, D), jnp.bfloat16),
+            pltpu.SemaphoreType.DMA((5,)),
         ],
         compiler_params=pltpu.CompilerParams(vmem_limit_bytes=20 * MIB),
         cost_estimate=pl.CostEstimate(
             flops=2 * 2 * TOK * EXPERTS * c * D * 2, bytes_accessed=EXPERTS * c * D * 2, transcendentals=0
         ),
         name="combine_last_slots",
-    )(late, in_hbm(sums), y)
+    )(in_hbm(late), in_hbm(sums), y)
 
 
 def exchange(wire):

time: 246 us -> 245 us (level)
  no operation moved by 1% of the time
where the time goes in v5:
time: 245 us
  blocking collectives  97.9 us (40%)
  waiting for transfers between devices  66.2 us (27%)
  Pallas kernels  65.2 us (27%)
  starting transfers between devices  15.3 us (6%)
    all_to_all x1, blocking collectives, exchange(): lax.all_to_all(blocks, AXES, split_axis=0, concat_axis=0, tiled=True)  97.9 us
    all_to_all x3, waiting for transfers between devices, exchange(): lax.all_to_all(blocks, AXES, split_axis=0, concat_axis=0, tiled=True)  66.2 us
    pallas_call x2, Pallas kernels, ffn(): pl.pallas_call(functools.partial(ffn_kernel, c), in_specs=[pl.BlockSpec(m...  50.2 us
    all_to_all x3, starting transfers between devices, exchange(): lax.all_to_all(blocks, AXES, split_axis=0, concat_axis=0, tiled=True)  15.3 us
    pallas_call x1, Pallas kernels, first_combine(): pl.pallas_call(first_combine_kernel, in_specs=[vmem] * 3, out_specs=(vmem...  6 us
    pallas_call x1, Pallas kernels, pack(): pl.pallas_call(pack_kernel, in_specs=[any_spec] * 3, out_specs=[vmem for...  5.74 us
  transfers between devices with their start and end apart: 3, of which 3 were waited for; matrix products, arithmetic and copies ran while one was open for 0% of the time, Pallas kernels for 23%

profile of v5, /device:TPU:1, one launch (start us, length us, event | category | flops | bytes accessed | tf_op | source)
XLA Modules:
  0.0 244.9 jit_solution(13939039659352488163)
XLA Ops:
  0.0 5.7 %pack_slots.1 = (bf16[1024,3584]{1,0:T(8,128)(2,1)S(1)}, bf16[1024,1792]{1,0:T(8,128)(2,1)S(1)}) custom-call(s32[8,128]{1,0:T(8,128)} %bitcast.16, bf16[128,3584]{1,0:T(8,128)(2,1)} %tokens_hbm.1, bf16[128,3584]{1,0:T(8,128)(2,1)} %grads_hbm.1), custom_call_target="tpu_custom_call" | custom-call | flops 3758096384 | bytes 11010048 | tf_op jit(solution)/shard_map/pack_slots/pallas_call | solution.py:93
  5.8 0.0 copy-start
  5.8 97.9 %all_to_all.20 = bf16[128,8,3584]{2,1,0:T(8,128)(2,1)} all-to-all(bf16[128,8,3584]{2,1,0:T(8,128)(2,1)S(1)} %bitcast.13), channel_id=1, replica_groups=mesh['node'=16,'local'=8] {'node','local'}, dimensions={0} | all-to-all | bytes 14680064 | tf_op jit(solution)/shard_map/all_to_all | solution.py:331
  103.6 0.0 copy-done
  103.6 5.7 %all-to-all-start.2 = ((bf16[128,8,1792]{2,1,0:T(8,128)(2,1)}), bf16[128,8,1792]{2,1,0:T(8,128)(2,1)}, u32[]{:S(2)}, u32[]{:S(2)}) async-start(bf16[128,8,1792]{2,1,0:T(8,128)(2,1)} %bitcast.15), calls=%async_computation.2 | async-start | bytes 7340032 | tf_op jit(solution)/shard_map/all_to_all | solution.py:331
  109.3 31.1 %expert_gradients.2 = bf16[1024,1792]{1,0:T(8,128)(2,1)} custom-call(bf16[1024,3584]{1,0:T(8,128)(2,1)} %bitcast.19, bf16[3584,1024]{1,0:T(8,128)(2,1)} %bitcast.22, bf16[3584,1024]{1,0:T(8,128)(2,1)} %bitcast.24, bf16[1024,3584]{1,0:T(8,128)(2,1)} %bitcast.26), custom_call_target="tpu_custom_call" | custom-call | flops 18790481920 | bytes 22020096 | tf_op jit(solution)/shard_map/expert_gradients/pallas_call | solution.py:199
  140.4 16.2 %all-to-all-done.2 = bf16[128,8,1792]{2,1,0:T(8,128)(2,1)} async-done(((bf16[128,8,1792]{2,1,0:T(8,128)(2,1)}), bf16[128,8,1792]{2,1,0:T(8,128)(2,1)}, u32[]{:S(2)}, u32[]{:S(2)}) %all-to-all-start.2) | async-done | bytes 3670048 | tf_op jit(solution)/shard_map/all_to_all | solution.py:331
  156.6 5.4 %all-to-all-start.1 = ((bf16[128,8,1792]{2,1,0:T(8,128)(2,1)}), bf16[128,8,1792]{2,1,0:T(8,128)(2,1)}, u32[]{:S(2)}, u32[]{:S(2)}) async-start(bf16[128,8,1792]{2,1,0:T(8,128)(2,1)} %bitcast.20), calls=%async_computation.1 | async-start | bytes 7340032 | tf_op jit(solution)/shard_map/all_to_all | solution.py:331
  162.0 19.2 %expert_gradients.3 = bf16[1024,896]{1,0:T(8,128)(2,1)} custom-call(bf16[1024,1792]{1,0:T(8,128)(2,1)} %bitcast.10.wire_ref, bf16[3584,1024]{1,0:T(8,128)(2,1)} %bitcast.23, bf16[3584,1024]{1,0:T(8,128)(2,1)} %bitcast.25, bf16[1024,3584]{1,0:T(8,128)(2,1)} %bitcast.27), custom_call_target="tpu_custom_call" | custom-call | flops 9395240960 | bytes 22020096 | tf_op jit(solution)/shard_map/expert_gradients/pallas_call | solution.py:199
  181.1 0.0 copy-start.1
  181.1 0.0 copy-start.2
  181.1 28.1 %all-to-all-done.1 = bf16[128,8,1792]{2,1,0:T(8,128)(2,1)} async-done(((bf16[128,8,1792]{2,1,0:T(8,128)(2,1)}), bf16[128,8,1792]{2,1,0:T(8,128)(2,1)}, u32[]{:S(2)}, u32[]{:S(2)}) %all-to-all-start.1) | async-done | bytes 3670048 | tf_op jit(solution)/shard_map/all_to_all | solution.py:331
  209.2 4.3 %all-to-all-start.3 = ((bf16[128,8,896]{2,1,0:T(8,128)(2,1)}), bf16[128,8,896]{2,1,0:T(8,128)(2,1)S(1)}, u32[]{:S(2)}, u32[]{:S(2)}) async-start(bf16[128,8,896]{2,1,0:T(8,128)(2,1)} %bitcast.21), calls=%async_computation.3 | async-start | bytes 3670016 | tf_op jit(solution)/shard_map/all_to_all | solution.py:331
  213.5 0.0 copy-done.1
  213.5 0.0 copy-done.2
  213.6 6.0 %combine_first_slots.1 = (f32[128,3584]{1,0:T(8,128)}, bf16[256,256]{1,0:T(8,128)(2,1)}) custom-call(s32[8,128]{1,0:T(8,128)S(1)} %bitcast.17, f32[8,128]{1,0:T(8,128)S(1)} %bitcast.18, bf16[1024,1792]{1,0:T(8,128)(2,1)} %bitcast.8.y_ref), custom_call_target="tpu_custom_call" | custom-call | flops 1879048192 | bytes 3670016 | tf_op jit(solution)/shard_map/combine_first_slots/pallas_call | solution.py:289
  219.6 21.9 %all-to-all-done.3 = bf16[128,8,896]{2,1,0:T(8,128)(2,1)S(1)} async-done(((bf16[128,8,896]{2,1,0:T(8,128)(2,1)}), bf16[128,8,896]{2,1,0:T(8,128)(2,1)S(1)}, u32[]{:S(2)}, u32[]{:S(2)}) %all-to-all-start.3) | async-done | bytes 1835040 | tf_op jit(solution)/shard_map/all_to_all | solution.py:331
  241.4 3.2 %combine_last_slots.1 = bf16[128,3584]{1,0:T(8,128)(2,1)} custom-call(bf16[256,256]{1,0:T(8,128)(2,1)} %get-tuple-element.10.late_hbm, f32[128,3584]{1,0:T(8,128)} %get-tuple-element.11.sum_hbm, bf16[1024,896]{1,0:T(8,128)(2,1)S(1)} %bitcast.14), custom_call_target="tpu_custom_call" | custom-call | flops 939524096 | bytes 1835008 | tf_op jit(solution)/shard_map/combine_last_slots/pallas_call | solution.py:309
Async XLA Ops:
  5.8 97.9 %copy-start = (bf16[1024,1792]{1,0:T(8,128)(2,1)}, bf16[1024,1792]{1,0:T(8,128)(2,1)S(1)}, u32[]{:S(2)}) copy-start(bf16[1024,1792]{1,0:T(8,128)(2,1)S(1)} %get-tuple-element.12) | copy-start | bytes 11010052
  103.6 52.9 %all-to-all-start.2 = ((bf16[128,8,1792]{2,1,0:T(8,128)(2,1)}), bf16[128,8,1792]{2,1,0:T(8,128)(2,1)}, u32[]{:S(2)}, u32[]{:S(2)}) async-start(bf16[128,8,1792]{2,1,0:T(8,128)(2,1)} %bitcast.15), calls=%async_computation.2 | async-start | bytes 7340032 | tf_op jit(solution)/shard_map/all_to_all | solution.py:331
  156.6 52.6 %all-to-all-start.1 = ((bf16[128,8,1792]{2,1,0:T(8,128)(2,1)}), bf16[128,8,1792]{2,1,0:T(8,128)(2,1)}, u32[]{:S(2)}, u32[]{:S(2)}) async-start(bf16[128,8,1792]{2,1,0:T(8,128)(2,1)} %bitcast.20), calls=%async_computation.1 | async-start | bytes 7340032 | tf_op jit(solution)/shard_map/all_to_all | solution.py:331
  181.1 32.4 %copy-start.1 = (s32[128,8]{0,1:T(8,128)S(1)}, s32[128,8]{0,1:T(8,128)}, u32[]{:S(2)}) copy-start(s32[128,8]{0,1:T(8,128)} %param.9) | copy-start | bytes 12292
  181.1 32.4 %copy-start.2 = (f32[128,8]{0,1:T(8,128)S(1)}, f32[128,8]{0,1:T(8,128)}, u32[]{:S(2)}) copy-start(f32[128,8]{0,1:T(8,128)} %param.10) | copy-start | bytes 12292
  209.2 32.2 %all-to-all-start.3 = ((bf16[128,8,896]{2,1,0:T(8,128)(2,1)}), bf16[128,8,896]{2,1,0:T(8,128)(2,1)S(1)}, u32[]{:S(2)}, u32[]{:S(2)}) async-start(bf16[128,8,896]{2,1,0:T(8,128)(2,1)} %bitcast.21), calls=%async_computation.3 | async-start | bytes 3670016 | tf_op jit(solution)/shard_map/all_to_all | solution.py:331

commit v6 on v5

--- a/solution.py
+++ b/solution.py
@@ -262,22 +262,22 @@
 
 
 def last_combine_kernel(late_hbm, sum_hbm, y_ref, out_hbm, late, sums, rows_ref, out, sems):
-    halves = [pl.ds(h * D // 2, D // 2) for h in range(2)]
+    quarters = [pl.ds(q * UNIT, UNIT) for q in range(4)]
     load_late = pltpu.make_async_copy(late_hbm, late, sems.at[0])
     loads = [
-        pltpu.make_async_copy(sum_hbm.at[:, cols], sums.at[:, cols], sems.at[1 + h])
-        for h, cols in enumerate(halves)
+        pltpu.make_async_copy(sum_hbm.at[:, cols], sums.at[:, cols], sems.at[1 + q])
+        for q, cols in enumerate(quarters)
     ]
     for copy in (load_late, *loads):
         copy.start()
     slot_rows(PARTS[1][0], y_ref, rows_ref)
     load_late.wait()
     stores = []
-    for h, cols in enumerate(halves):
+    for q, cols in enumerate(quarters):
         total = jnp.dot(late[...], rows_ref[:, cols], preferred_element_type=jnp.float32)
-        loads[h].wait()
+        loads[q].wait()
         out[:, cols] = (sums[:, cols] + total[:TOK] + total[TOK:]).astype(jnp.bfloat16)
-        stores.append(pltpu.make_async_copy(out.at[:, cols], out_hbm.at[:, cols], sems.at[3 + h]))
+        stores.append(pltpu.make_async_copy(out.at[:, cols], out_hbm.at[:, cols], sems.at[5 + q]))
         stores[-1].start()
     for copy in stores:
         copy.wait()
@@ -316,7 +316,7 @@
             pltpu.VMEM((TOK, D), jnp.float32),
             pltpu.VMEM((EXPERTS * c, D), jnp.bfloat16),
             pltpu.VMEM((TOK, D), jnp.bfloat16),
-            pltpu.SemaphoreType.DMA((5,)),
+            pltpu.SemaphoreType.DMA((9,)),
         ],
         compiler_params=pltpu.CompilerParams(vmem_limit_bytes=20 * MIB),
         cost_estimate=pl.CostEstimate(

time: 245 us -> 246 us (level)
  no operation moved by 1% of the time
where the time goes in v6:
time: 246 us; the launch traced here: 245 us
  blocking collectives  97.9 us (40%)
  waiting for transfers between devices  66.2 us (27%)
  Pallas kernels  65.4 us (27%)
  starting transfers between devices  15.3 us (6%)
    all_to_all x1, blocking collectives, exchange(): lax.all_to_all(blocks, AXES, split_axis=0, concat_axis=0, tiled=True)  97.9 us
    all_to_all x3, waiting for transfers between devices, exchange(): lax.all_to_all(blocks, AXES, split_axis=0, concat_axis=0, tiled=True)  66.2 us
    pallas_call x2, Pallas kernels, ffn(): pl.pallas_call(functools.partial(ffn_kernel, c), in_specs=[pl.BlockSpec(m...  50.2 us
    all_to_all x3, starting transfers between devices, exchange(): lax.all_to_all(blocks, AXES, split_axis=0, concat_axis=0, tiled=True)  15.3 us
    pallas_call x1, Pallas kernels, first_combine(): pl.pallas_call(first_combine_kernel, in_specs=[vmem] * 3, out_specs=(vmem...  6 us
    pallas_call x1, Pallas kernels, pack(): pl.pallas_call(pack_kernel, in_specs=[any_spec] * 3, out_specs=[vmem for...  5.74 us
  transfers between devices with their start and end apart: 3, of which 3 were waited for; matrix products, arithmetic and copies ran while one was open for 0% of the time, Pallas kernels for 23%

profile of v6, /device:TPU:1, one launch (start us, length us, event | category | flops | bytes accessed | tf_op | source)
XLA Modules:
  0.0 245.0 jit_solution(7045270358303676771)
XLA Ops:
  0.0 5.7 %pack_slots.1 = (bf16[1024,3584]{1,0:T(8,128)(2,1)S(1)}, bf16[1024,1792]{1,0:T(8,128)(2,1)S(1)}) custom-call(s32[8,128]{1,0:T(8,128)} %bitcast.16, bf16[128,3584]{1,0:T(8,128)(2,1)} %tokens_hbm.1, bf16[128,3584]{1,0:T(8,128)(2,1)} %grads_hbm.1), custom_call_target="tpu_custom_call" | custom-call | flops 3758096384 | bytes 11010048 | tf_op jit(solution)/shard_map/pack_slots/pallas_call | solution.py:93
  5.8 0.0 copy-start
  5.8 97.9 %all_to_all.20 = bf16[128,8,3584]{2,1,0:T(8,128)(2,1)} all-to-all(bf16[128,8,3584]{2,1,0:T(8,128)(2,1)S(1)} %bitcast.13), channel_id=1, replica_groups=mesh['node'=16,'local'=8] {'node','local'}, dimensions={0} | all-to-all | bytes 14680064 | tf_op jit(solution)/shard_map/all_to_all | solution.py:331
  103.6 0.0 copy-done
  103.6 5.7 %all-to-all-start.2 = ((bf16[128,8,1792]{2,1,0:T(8,128)(2,1)}), bf16[128,8,1792]{2,1,0:T(8,128)(2,1)}, u32[]{:S(2)}, u32[]{:S(2)}) async-start(bf16[128,8,1792]{2,1,0:T(8,128)(2,1)} %bitcast.15), calls=%async_computation.2 | async-start | bytes 7340032 | tf_op jit(solution)/shard_map/all_to_all | solution.py:331
  109.3 31.1 %expert_gradients.2 = bf16[1024,1792]{1,0:T(8,128)(2,1)} custom-call(bf16[1024,3584]{1,0:T(8,128)(2,1)} %bitcast.19, bf16[3584,1024]{1,0:T(8,128)(2,1)} %bitcast.22, bf16[3584,1024]{1,0:T(8,128)(2,1)} %bitcast.24, bf16[1024,3584]{1,0:T(8,128)(2,1)} %bitcast.26), custom_call_target="tpu_custom_call" | custom-call | flops 18790481920 | bytes 22020096 | tf_op jit(solution)/shard_map/expert_gradients/pallas_call | solution.py:199
  140.4 16.2 %all-to-all-done.2 = bf16[128,8,1792]{2,1,0:T(8,128)(2,1)} async-done(((bf16[128,8,1792]{2,1,0:T(8,128)(2,1)}), bf16[128,8,1792]{2,1,0:T(8,128)(2,1)}, u32[]{:S(2)}, u32[]{:S(2)}) %all-to-all-start.2) | async-done | bytes 3670048 | tf_op jit(solution)/shard_map/all_to_all | solution.py:331
  156.6 5.4 %all-to-all-start.1 = ((bf16[128,8,1792]{2,1,0:T(8,128)(2,1)}), bf16[128,8,1792]{2,1,0:T(8,128)(2,1)}, u32[]{:S(2)}, u32[]{:S(2)}) async-start(bf16[128,8,1792]{2,1,0:T(8,128)(2,1)} %bitcast.20), calls=%async_computation.1 | async-start | bytes 7340032 | tf_op jit(solution)/shard_map/all_to_all | solution.py:331
  162.0 19.2 %expert_gradients.3 = bf16[1024,896]{1,0:T(8,128)(2,1)} custom-call(bf16[1024,1792]{1,0:T(8,128)(2,1)} %bitcast.10.wire_ref, bf16[3584,1024]{1,0:T(8,128)(2,1)} %bitcast.23, bf16[3584,1024]{1,0:T(8,128)(2,1)} %bitcast.25, bf16[1024,3584]{1,0:T(8,128)(2,1)} %bitcast.27), custom_call_target="tpu_custom_call" | custom-call | flops 9395240960 | bytes 22020096 | tf_op jit(solution)/shard_map/expert_gradients/pallas_call | solution.py:199
  181.1 0.0 copy-start.1
  181.1 0.0 copy-start.2
  181.1 28.1 %all-to-all-done.1 = bf16[128,8,1792]{2,1,0:T(8,128)(2,1)} async-done(((bf16[128,8,1792]{2,1,0:T(8,128)(2,1)}), bf16[128,8,1792]{2,1,0:T(8,128)(2,1)}, u32[]{:S(2)}, u32[]{:S(2)}) %all-to-all-start.1) | async-done | bytes 3670048 | tf_op jit(solution)/shard_map/all_to_all | solution.py:331
  209.2 4.3 %all-to-all-start.3 = ((bf16[128,8,896]{2,1,0:T(8,128)(2,1)}), bf16[128,8,896]{2,1,0:T(8,128)(2,1)S(1)}, u32[]{:S(2)}, u32[]{:S(2)}) async-start(bf16[128,8,896]{2,1,0:T(8,128)(2,1)} %bitcast.21), calls=%async_computation.3 | async-start | bytes 3670016 | tf_op jit(solution)/shard_map/all_to_all | solution.py:331
  213.5 0.0 copy-done.1
  213.5 0.0 copy-done.2
  213.6 6.0 %combine_first_slots.1 = (f32[128,3584]{1,0:T(8,128)}, bf16[256,256]{1,0:T(8,128)(2,1)}) custom-call(s32[8,128]{1,0:T(8,128)S(1)} %bitcast.17, f32[8,128]{1,0:T(8,128)S(1)} %bitcast.18, bf16[1024,1792]{1,0:T(8,128)(2,1)} %bitcast.8.y_ref), custom_call_target="tpu_custom_call" | custom-call | flops 1879048192 | bytes 3670016 | tf_op jit(solution)/shard_map/combine_first_slots/pallas_call | solution.py:289
  219.6 21.9 %all-to-all-done.3 = bf16[128,8,896]{2,1,0:T(8,128)(2,1)S(1)} async-done(((bf16[128,8,896]{2,1,0:T(8,128)(2,1)}), bf16[128,8,896]{2,1,0:T(8,128)(2,1)S(1)}, u32[]{:S(2)}, u32[]{:S(2)}) %all-to-all-start.3) | async-done | bytes 1835040 | tf_op jit(solution)/shard_map/all_to_all | solution.py:331
  241.4 3.4 %combine_last_slots.1 = bf16[128,3584]{1,0:T(8,128)(2,1)} custom-call(bf16[256,256]{1,0:T(8,128)(2,1)} %get-tuple-element.10.late_hbm, f32[128,3584]{1,0:T(8,128)} %get-tuple-element.11.sum_hbm, bf16[1024,896]{1,0:T(8,128)(2,1)S(1)} %bitcast.14), custom_call_target="tpu_custom_call" | custom-call | flops 939524096 | bytes 1835008 | tf_op jit(solution)/shard_map/combine_last_slots/pallas_call | solution.py:309
Async XLA Ops:
  5.8 97.9 %copy-start = (bf16[1024,1792]{1,0:T(8,128)(2,1)}, bf16[1024,1792]{1,0:T(8,128)(2,1)S(1)}, u32[]{:S(2)}) copy-start(bf16[1024,1792]{1,0:T(8,128)(2,1)S(1)} %get-tuple-element.12) | copy-start | bytes 11010052
  103.6 52.9 %all-to-all-start.2 = ((bf16[128,8,1792]{2,1,0:T(8,128)(2,1)}), bf16[128,8,1792]{2,1,0:T(8,128)(2,1)}, u32[]{:S(2)}, u32[]{:S(2)}) async-start(bf16[128,8,1792]{2,1,0:T(8,128)(2,1)} %bitcast.15), calls=%async_computation.2 | async-start | bytes 7340032 | tf_op jit(solution)/shard_map/all_to_all | solution.py:331
  156.6 52.6 %all-to-all-start.1 = ((bf16[128,8,1792]{2,1,0:T(8,128)(2,1)}), bf16[128,8,1792]{2,1,0:T(8,128)(2,1)}, u32[]{:S(2)}, u32[]{:S(2)}) async-start(bf16[128,8,1792]{2,1,0:T(8,128)(2,1)} %bitcast.20), calls=%async_computation.1 | async-start | bytes 7340032 | tf_op jit(solution)/shard_map/all_to_all | solution.py:331
  181.1 32.4 %copy-start.1 = (s32[128,8]{0,1:T(8,128)S(1)}, s32[128,8]{0,1:T(8,128)}, u32[]{:S(2)}) copy-start(s32[128,8]{0,1:T(8,128)} %param.9) | copy-start | bytes 12292
  181.1 32.4 %copy-start.2 = (f32[128,8]{0,1:T(8,128)S(1)}, f32[128,8]{0,1:T(8,128)}, u32[]{:S(2)}) copy-start(f32[128,8]{0,1:T(8,128)} %param.10) | copy-start | bytes 12292
  209.2 32.2 %all-to-all-start.3 = ((bf16[128,8,896]{2,1,0:T(8,128)(2,1)}), bf16[128,8,896]{2,1,0:T(8,128)(2,1)S(1)}, u32[]{:S(2)}, u32[]{:S(2)}) async-start(bf16[128,8,896]{2,1,0:T(8,128)(2,1)} %bitcast.21), calls=%async_computation.3 | async-start | bytes 3670016 | tf_op jit(solution)/shard_map/all_to_all | solution.py:331
